TPU v7x, 32 devices: a whole 2x2x4 slice. The times are simulated.
32 devices in a mesh: lat: 2 (over x), lon: 4 (over y, core), mem: 4 (over z).
Axes of the slice: x: 2, y: 2, z: 4, core: 2. Of those that a mesh axis runs over, the one named last changes fastest.
Arguments:
- perturbations: bfloat16 [32, 128, 1024], P('mem', 'lat', 'lon'), may hold values from -6 to 6
- diffusivity: float32 [128, 1024], P('lat', 'lon'), may hold values from 0.19 to 0.249
- sea_mask: int32 [128, 1024], P('lat', 'lon'), may hold values from 0 to 1
- obs_owner: int32 [65536, 1], P(('lat', 'lon', 'mem')), may hold values from 0 to 7; in each aligned block of 2048 rows (0 to 2047, 2048 to 4095, ...) at most 512 rows name the same one
- obs_cell: int32 [65536], P(('lat', 'lon', 'mem')), may hold values from 0 to 16383
- obs_depart: float32 [65536], P(('lat', 'lon', 'mem')), may hold values from -6 to 6
- obs_weight: float32 [65536], P(('lat', 'lon', 'mem')), may hold values from 0.25 to 2
Outputs:
- increment: float32 [128, 1024], P('lat', 'lon')
- obs_residual: float32 [65536], P(('lat', 'lon', 'mem'))
Inputs may be any that keep to these rules, and one draw needn't show every extreme that they name: `obs_owner`: within each device's aligned block of 2048 rows no tile is named by more than 512 rows, a bound that some block reaches.
All inputs are finite; a program needn't handle non-finite values.
Results may differ from a plain program's by a relative error of at most 0.0003.
Values sent between devices are 32-bit elements; how exact they have to be, the bound alone decides.
A program may use at most 64 MiB of HBM per device.

v0:
```python
import jax
import jax.numpy as jnp
from jax import lax
from jax.sharding import PartitionSpec as P

STEPS = 4


def extended(array, sides, width):
    for axis, dim in sides:
        size, length = (lax.axis_size(axis), array.shape[dim])
        up = [(i, (i + 1) % size) for i in range(size)]
        down = [(j, i) for i, j in up]
        last = lax.slice_in_dim(array, length - width, length, axis=dim)
        first = lax.slice_in_dim(array, 0, width, axis=dim)
        before = lax.ppermute(last, axis, up)
        after = lax.ppermute(first, axis, down)
        array = jnp.concatenate([before, array, after], axis=dim)
    return array


def face_weights(rate_padded, sea_padded):
    north_face = 0.5 * (rate_padded[:-1] + rate_padded[1:]) * sea_padded[:-1] * sea_padded[1:]
    east_face = (
        0.5 * (rate_padded[:, :-1] + rate_padded[:, 1:]) * sea_padded[:, :-1] * sea_padded[:, 1:]
    )
    return (north_face, east_face)


def diffuse_once(padded, north_face, east_face):
    centre = padded[:, 1:-1, 1:-1]
    result = centre + north_face[1:, 1:-1] * (padded[:, 2:, 1:-1] - centre)
    result = result - north_face[:-1, 1:-1] * (centre - padded[:, :-2, 1:-1])
    result = result + east_face[1:-1, 1:] * (padded[:, 1:-1, 2:] - centre)
    return result - east_face[1:-1, :-1] * (centre - padded[:, 1:-1, :-2])


def member_total(partial_value):
    return lax.psum(partial_value, "mem")


def covariance(source, member_values, north_face, east_face, sea_cover, divisor):
    spread = member_values * source[None]
    for sweep_index in range(STEPS):
        padded = extended(spread, (("lat", 1), ("lon", 2)), 1)
        spread = diffuse_once(padded, north_face, east_face)
    partial_value = jnp.sum(member_values * spread, axis=0)
    return sea_cover * member_total(partial_value) / divisor


def per_device(perturbations, diffusivity, sea_mask, obs_owner, obs_cell, obs_depart, obs_weight):
    members, tile_rows, tile_cols = perturbations.shape
    divisor = members * lax.axis_size("mem") - 1
    sea_cover = sea_mask.astype(jnp.float32)
    rim_width = 1
    stacked = jnp.stack([diffusivity, sea_cover])
    padded_coef = extended(stacked, (("lat", 1), ("lon", 2)), rim_width)
    lat_index = lax.axis_index("lat")
    row_ids = jnp.arange(tile_rows + 2 * rim_width)
    outside = (row_ids < rim_width) & (lat_index == 0) | (row_ids >= tile_rows + rim_width) & (
        lat_index == lax.axis_size("lat") - 1
    )
    sea_padded = jnp.where(outside[:, None], 0.0, padded_coef[1])
    north_face, east_face = face_weights(padded_coef[0], sea_padded)
    member_values = perturbations.astype(jnp.float32)
    obs_dest = obs_owner[:, 0]
    places = lax.axis_size("lat") * lax.axis_size("lon")
    capacity = max(2, 2 * obs_dest.shape[0] // places)
    matches = (obs_dest[:, None] == jnp.arange(places, dtype=jnp.int32)[None, :]).astype(jnp.int32)
    bucket_rank = jnp.sum((jnp.cumsum(matches, axis=0) - 1) * matches, axis=1)
    send_slot = obs_dest * capacity + bucket_rank
    outgoing = (
        jnp.zeros((2, places * capacity), jnp.float32)
        .at[:, send_slot]
        .set(jnp.stack([obs_depart, obs_weight]))
    )
    cell_slots = jnp.zeros((1, places * capacity), jnp.int32).at[0, send_slot].set(obs_cell)
    got_values, got_cells = (
        lax.all_to_all(outgoing, ("lat", "lon"), split_axis=1, concat_axis=1, tiled=True),
        lax.all_to_all(cell_slots, ("lat", "lon"), split_axis=1, concat_axis=1, tiled=True),
    )
    got_depart = got_values[0]
    got_weight = got_values[1]
    got_cell = got_cells[0]
    tile_cells = tile_rows * tile_cols
    innovation_part = jax.ops.segment_sum(
        got_weight * got_depart, got_cell, num_segments=tile_cells
    ).reshape(tile_rows, tile_cols)
    innovation = member_total(innovation_part)
    first_pass = covariance(innovation, member_values, north_face, east_face, sea_cover, divisor)
    at_obs = first_pass.reshape(-1)[got_cell]
    removed_part = jax.ops.segment_sum(
        got_weight * at_obs, got_cell, num_segments=tile_cells
    ).reshape(tile_rows, tile_cols)
    corrected = member_total(innovation_part - removed_part)
    increment = covariance(corrected, member_values, north_face, east_face, sea_cover, divisor)
    answer = got_depart - increment.reshape(-1)[got_cell]
    returned = lax.all_to_all(
        answer[None], ("lat", "lon"), split_axis=1, concat_axis=1, tiled=True
    )[0]
    obs_residual = returned[send_slot]
    return (increment, obs_residual)


def solution(mesh):
    return jax.shard_map(
        per_device,
        mesh=mesh,
        in_specs=(
            P("mem", "lat", "lon"),
            P("lat", "lon"),
            P("lat", "lon"),
            P(("lat", "lon", "mem"), None),
            P(("lat", "lon", "mem")),
            P(("lat", "lon", "mem")),
            P(("lat", "lon", "mem")),
        ),
        out_specs=(P("lat", "lon"), P(("lat", "lon", "mem"))),
        check_vma=False,
    )
```

profile of v0, /device:TPU:0, one launch (start us, length us, event | category | flops | bytes accessed | tf_op | source)
XLA Modules:
  0.0 441.8 jit_solution(2864864464777676505)
XLA Ops:
  13.3 6.1 %scatter_custom_fusion = f32[2,4096]{0,1:T(8,128)S(1)} fusion(s32[2048]{0:T(1024)S(1)} %bitcast.60, f32[2048,2]{1,0:T(8,128)S(1)} %copy.11, f32[]{:T(128)} %constant.12.clone.1), kind=kCustom, calls=%fused_computation.7 | custom fusion | bytes 32772 | tf_op jit(solution)/shard_map/scatter | solution.py:75
  20.7 5.2 %all-to-all-start.1 = ((f32[2,8,512]{2,0,1:T(2,128)}), f32[2,8,512]{2,0,1:T(2,128)S(1)}, u32[]{:S(2)}, u32[]{:S(2)}) async-start(f32[2,8,512]{2,0,1:T(2,128)} %copy.12), calls=%async_computation.1 | async-start | bytes 65536 | tf_op jit(solution)/shard_map/all_to_all | solution.py:79
  32.2 8.8 %scatter_custom_fusion.3 = s32[4096]{0:T(1024)} fusion(s32[2048]{0:T(1024)S(1)} %broadcast_select_fusion, s32[2048]{0:T(1024)} %param.11, s32[]{:T(128)} %constant.13.clone.1), kind=kCustom, calls=%fused_computation.220 | custom fusion | bytes 16896
  41.3 3.3 all-to-all-start
  44.8 4.5 %all-to-all-done = s32[1,8,512]{2,0,1:T(1,128)S(1)} async-done(((s32[1,8,512]{2,0,1:T(1,128)}), s32[1,8,512]{2,0,1:T(1,128)S(1)}, u32[]{:S(2)}, u32[]{:S(2)}) %all-to-all-start) | async-done | bytes 16416 | tf_op jit(solution)/shard_map/all_to_all | solution.py:80
  49.3 26.3 %scatter_custom_fusion.1 = f32[16384]{0:T(1024)S(1)} fusion(s32[4096]{0:T(1024)S(1)} %bitcast.64, f32[4096]{0:T(1024)S(1)} %mul.121, f32[]{:T(128)} %constant.12.clone.1), kind=kCustom, calls=%fused_computation.212 | custom fusion | flops 4096 | bytes 65540 | tf_op jit(solution)/shard_map/scatter-add | solution.py:86
  76.3 34.1 %all-reduce.6.cloned.1.call-done = f32[64,256]{1,0:T(8,128)} async-done(((f32[64,256]{1,0:T(8,128)}), f32[64,256]{1,0:T(8,128)}) %all-reduce.6.cloned.1.call-update) | async-done | bytes 65552 | tf_op jit(solution)/shard_map/psum | solution.py:39
  118.7 5.6 %collective-permute-done.7 = f32[8,66,1]{2,1,0:T(8,128)S(1)} collective-permute-done((f32[8,66,1]{2,1,0:T(8,128)S(1)}, f32[8,66,1]{2,1,0:T(8,128)S(1)}, u32[]{:S(2)}, u32[]{:S(2)}) %collective-permute-start.7) | collective-permute-done | bytes 2144 | tf_op jit(solution)/shard_map/ppermute | solution.py:16
  131.9 5.5 %collective-permute-done.11 = f32[8,66,1]{2,1,0:T(8,128)S(1)} collective-permute-done((f32[8,66,1]{2,1,0:T(8,128)S(1)}, f32[8,66,1]{2,1,0:T(8,128)S(1)}, u32[]{:S(2)}, u32[]{:S(2)}) %collective-permute-start.11) | collective-permute-done | bytes 2144 | tf_op jit(solution)/shard_map/ppermute | solution.py:16
  146.5 5.3 %collective-permute-done.15 = f32[8,66,1]{2,1,0:T(8,128)S(1)} collective-permute-done((f32[8,66,1]{2,1,0:T(8,128)S(1)}, f32[8,66,1]{2,1,0:T(8,128)S(1)}, u32[]{:S(2)}, u32[]{:S(2)}) %collective-permute-start.15) | collective-permute-done | bytes 2144 | tf_op jit(solution)/shard_map/ppermute | solution.py:16
  160.3 5.0 %collective-permute-done.19 = f32[8,66,1]{2,1,0:T(8,128)S(1)} collective-permute-done((f32[8,66,1]{2,1,0:T(8,128)S(1)}, f32[8,66,1]{2,1,0:T(8,128)S(1)}, u32[]{:S(2)}, u32[]{:S(2)}) %collective-permute-start.19) | collective-permute-done | bytes 2144 | tf_op jit(solution)/shard_map/ppermute | solution.py:16
  169.0 34.4 %all-reduce.8.cloned.1.call-done = f32[64,256]{1,0:T(8,128)} async-done(((f32[64,256]{1,0:T(8,128)}), f32[64,256]{1,0:T(8,128)}) %all-reduce.8.cloned.1.call-update) | async-done | bytes 65552 | tf_op jit(solution)/shard_map/psum | solution.py:39
  204.3 23.0 %gather_fusion = f32[4096]{0:T(1024)S(1)} fusion(f32[16384]{0:T(1024)S(1)} %bitcast.49, s32[4096]{0:T(1024)S(1)} %broadcast_clamp_fusion), kind=kCustom, calls=%fused_computation | custom fusion | bytes 49152 | tf_op jit(solution)/shard_map/gather | solution.py:91
  227.3 26.3 %scatter_custom_fusion.2 = f32[16384]{0:T(1024)S(1)} fusion(s32[4096]{0:T(1024)S(1)} %bitcast.66, f32[4096]{0:T(1024)S(1)} %mul.308, f32[]{:T(128)} %constant.12.clone.1), kind=kCustom, calls=%fused_computation.210 | custom fusion | flops 4096 | bytes 65540 | tf_op jit(solution)/shard_map/scatter-add | solution.py:92
  254.4 34.4 %all-reduce.10.cloned.1.call-done = f32[64,256]{1,0:T(8,128)} async-done(((f32[64,256]{1,0:T(8,128)}), f32[64,256]{1,0:T(8,128)}) %all-reduce.10.cloned.1.call-update) | async-done | bytes 65552 | tf_op jit(solution)/shard_map/psum | solution.py:39
  296.9 5.7 %collective-permute-done.23 = f32[8,66,1]{2,1,0:T(8,128)S(1)} collective-permute-done((f32[8,66,1]{2,1,0:T(8,128)S(1)}, f32[8,66,1]{2,1,0:T(8,128)S(1)}, u32[]{:S(2)}, u32[]{:S(2)}) %collective-permute-start.23) | collective-permute-done | bytes 2144 | tf_op jit(solution)/shard_map/ppermute | solution.py:16
  310.3 5.5 %collective-permute-done.27 = f32[8,66,1]{2,1,0:T(8,128)S(1)} collective-permute-done((f32[8,66,1]{2,1,0:T(8,128)S(1)}, f32[8,66,1]{2,1,0:T(8,128)S(1)}, u32[]{:S(2)}, u32[]{:S(2)}) %collective-permute-start.27) | collective-permute-done | bytes 2144 | tf_op jit(solution)/shard_map/ppermute | solution.py:16
  324.8 5.3 %collective-permute-done.31 = f32[8,66,1]{2,1,0:T(8,128)S(1)} collective-permute-done((f32[8,66,1]{2,1,0:T(8,128)S(1)}, f32[8,66,1]{2,1,0:T(8,128)S(1)}, u32[]{:S(2)}, u32[]{:S(2)}) %collective-permute-start.31) | collective-permute-done | bytes 2144 | tf_op jit(solution)/shard_map/ppermute | solution.py:16
  338.6 5.1 %collective-permute-done.35 = f32[8,66,1]{2,1,0:T(8,128)S(1)} collective-permute-done((f32[8,66,1]{2,1,0:T(8,128)S(1)}, f32[8,66,1]{2,1,0:T(8,128)S(1)}, u32[]{:S(2)}, u32[]{:S(2)}) %collective-permute-start.35) | collective-permute-done | bytes 2144 | tf_op jit(solution)/shard_map/ppermute | solution.py:16
  347.1 34.7 %all-reduce.12.cloned.1.call-done = f32[64,256]{1,0:T(8,128)} async-done(((f32[64,256]{1,0:T(8,128)}), f32[64,256]{1,0:T(8,128)}) %all-reduce.12.cloned.1.call-update) | async-done | bytes 65552 | tf_op jit(solution)/shard_map/psum | solution.py:39
  382.6 23.0 %gather_fusion.1 = f32[4096]{0:T(1024)S(1)} fusion(f32[16384]{0:T(1024)S(1)} %bitcast.50, s32[4096]{0:T(1024)S(1)} %broadcast_clamp_fusion), kind=kCustom, calls=%fused_computation.1 | custom fusion | bytes 49152 | tf_op jit(solution)/shard_map/gather | solution.py:97
  406.3 3.7 all-to-all-start.2
  410.0 4.7 %all-to-all-done.2 = f32[1,8,512]{2,0,1:T(1,128)S(1)} async-done(((f32[1,8,512]{2,0,1:T(1,128)}), f32[1,8,512]{2,0,1:T(1,128)S(1)}, u32[]{:S(2)}, u32[]{:S(2)}) %all-to-all-start.2) | async-done | bytes 16416 | tf_op jit(solution)/shard_map/all_to_all | solution.py:98
  414.7 20.5 %gather_fusion.2 = f32[2048]{0:T(1024)} fusion(f32[4096]{0:T(1024)S(1)} %bitcast.51, s32[2048]{0:T(1024)S(1)} %broadcast_clamp_fusion.1), kind=kCustom, calls=%fused_computation.2 | custom fusion | bytes 24576 | tf_op jit(solution)/shard_map/gather | solution.py:101
  (161 shorter events, 91.3 us)
Async XLA Ops:
  20.7 20.6 %all-to-all-start.1 = ((f32[2,8,512]{2,0,1:T(2,128)}), f32[2,8,512]{2,0,1:T(2,128)S(1)}, u32[]{:S(2)}, u32[]{:S(2)}) async-start(f32[2,8,512]{2,0,1:T(2,128)} %copy.12), calls=%async_computation.1 | async-start | bytes 65536 | tf_op jit(solution)/shard_map/all_to_all | solution.py:79
  31.6 9.3 %collective-permute-start.3 = (f32[2,66,1]{2,1,0:T(8,128)S(1)}, f32[2,66,1]{2,1,0:T(8,128)S(1)}, u32[]{:S(2)}, u32[]{:S(2)}) collective-permute-start(f32[2,66,1]{2,1,0:T(8,128)S(1)} %get-tuple-element.35), channel_id=1, source_target_pairs={{4,0},{8,4},{12,8},{0,12},{5,1},{9,5},{13,9},{1,13},{6,2},{10,6},{... | collective-permute-start | bytes 1592 | tf_op jit(solution)/shard_map/ppermute | solution.py:17
  31.7 9.3 %collective-permute-start.2 = (f32[2,66,1]{2,1,0:T(8,128)S(1)}, f32[2,66,1]{2,1,0:T(8,128)S(1)}, u32[]{:S(2)}, u32[]{:S(2)}) collective-permute-start(f32[2,66,1]{2,1,0:T(8,128)S(1)} %get-tuple-element.34), channel_id=1, source_target_pairs={{0,4},{4,8},{8,12},{12,0},{1,5},{5,9},{9,13},{13,1},{2,6},{6,10},{... | collective-permute-start | bytes 1592 | tf_op jit(solution)/shard_map/ppermute | solution.py:16
  41.3 8.0 %all-to-all-start = ((s32[1,8,512]{2,0,1:T(1,128)}), s32[1,8,512]{2,0,1:T(1,128)S(1)}, u32[]{:S(2)}, u32[]{:S(2)}) async-start(s32[1,8,512]{2,0,1:T(1,128)} %bitcast.4), calls=%async_computation | async-start | bytes 32768 | tf_op jit(solution)/shard_map/all_to_all | solution.py:80
  44.7 65.8 %all-reduce.6.cloned.1.call-start = ((), (), s32[]{:S(2)}) async-start(), calls=%async_computation.3 | async-start | bytes 131072 | tf_op jit(solution)/shard_map/psum | solution.py:39
  76.2 127.1 %all-reduce.8.cloned.1.call-start = ((), (), s32[]{:S(2)}) async-start(), calls=%async_computation.4 | async-start | bytes 131072 | tf_op jit(solution)/shard_map/psum | solution.py:39
  116.7 7.5 %collective-permute-start.7 = (f32[8,66,1]{2,1,0:T(8,128)S(1)}, f32[8,66,1]{2,1,0:T(8,128)S(1)}, u32[]{:S(2)}, u32[]{:S(2)}) collective-permute-start(f32[8,66,1]{2,1,0:T(8,128)S(1)} %get-tuple-element.17), channel_id=1, source_target_pairs={{0,4},{4,8},{8,12},{12,0},{1,5},{5,9},{9,13},{13,1},{2,6},{6,10},{... | collective-permute-start | bytes 6344 | tf_op jit(solution)/shard_map/ppermute | solution.py:16
  116.8 8.3 %collective-permute-start.6 = (f32[8,66,1]{2,1,0:T(8,128)S(1)}, f32[8,66,1]{2,1,0:T(8,128)S(1)}, u32[]{:S(2)}, u32[]{:S(2)}) collective-permute-start(f32[8,66,1]{2,1,0:T(8,128)S(1)} %get-tuple-element.16), channel_id=1, source_target_pairs={{4,0},{8,4},{12,8},{0,12},{5,1},{9,5},{13,9},{1,13},{6,2},{10,6},{... | collective-permute-start | bytes 6344 | tf_op jit(solution)/shard_map/ppermute | solution.py:17
  130.1 7.3 %collective-permute-start.11 = (f32[8,66,1]{2,1,0:T(8,128)S(1)}, f32[8,66,1]{2,1,0:T(8,128)S(1)}, u32[]{:S(2)}, u32[]{:S(2)}) collective-permute-start(f32[8,66,1]{2,1,0:T(8,128)S(1)} %get-tuple-element.15), channel_id=1, source_target_pairs={{0,4},{4,8},{8,12},{12,0},{1,5},{5,9},{9,13},{13,1},{2,6},{6,10},{... | collective-permute-start | bytes 6344 | tf_op jit(solution)/shard_map/ppermute | solution.py:16
  130.2 8.5 %collective-permute-start.10 = (f32[8,66,1]{2,1,0:T(8,128)S(1)}, f32[8,66,1]{2,1,0:T(8,128)S(1)}, u32[]{:S(2)}, u32[]{:S(2)}) collective-permute-start(f32[8,66,1]{2,1,0:T(8,128)S(1)} %get-tuple-element.14), channel_id=1, source_target_pairs={{4,0},{8,4},{12,8},{0,12},{5,1},{9,5},{13,9},{1,13},{6,2},{10,6},{... | collective-permute-start | bytes 6344 | tf_op jit(solution)/shard_map/ppermute | solution.py:17
  144.7 7.1 %collective-permute-start.15 = (f32[8,66,1]{2,1,0:T(8,128)S(1)}, f32[8,66,1]{2,1,0:T(8,128)S(1)}, u32[]{:S(2)}, u32[]{:S(2)}) collective-permute-start(f32[8,66,1]{2,1,0:T(8,128)S(1)} %get-tuple-element.13), channel_id=1, source_target_pairs={{0,4},{4,8},{8,12},{12,0},{1,5},{5,9},{9,13},{13,1},{2,6},{6,10},{... | collective-permute-start | bytes 6344 | tf_op jit(solution)/shard_map/ppermute | solution.py:16
  144.7 8.7 %collective-permute-start.14 = (f32[8,66,1]{2,1,0:T(8,128)S(1)}, f32[8,66,1]{2,1,0:T(8,128)S(1)}, u32[]{:S(2)}, u32[]{:S(2)}) collective-permute-start(f32[8,66,1]{2,1,0:T(8,128)S(1)} %get-tuple-element.12), channel_id=1, source_target_pairs={{4,0},{8,4},{12,8},{0,12},{5,1},{9,5},{13,9},{1,13},{6,2},{10,6},{... | collective-permute-start | bytes 6344 | tf_op jit(solution)/shard_map/ppermute | solution.py:17
  158.5 6.9 %collective-permute-start.19 = (f32[8,66,1]{2,1,0:T(8,128)S(1)}, f32[8,66,1]{2,1,0:T(8,128)S(1)}, u32[]{:S(2)}, u32[]{:S(2)}) collective-permute-start(f32[8,66,1]{2,1,0:T(8,128)S(1)} %get-tuple-element.11), channel_id=1, source_target_pairs={{0,4},{4,8},{8,12},{12,0},{1,5},{5,9},{9,13},{13,1},{2,6},{6,10},{... | collective-permute-start | bytes 6344 | tf_op jit(solution)/shard_map/ppermute | solution.py:16
  158.5 8.9 %collective-permute-start.18 = (f32[8,66,1]{2,1,0:T(8,128)S(1)}, f32[8,66,1]{2,1,0:T(8,128)S(1)}, u32[]{:S(2)}, u32[]{:S(2)}) collective-permute-start(f32[8,66,1]{2,1,0:T(8,128)S(1)} %get-tuple-element.10), channel_id=1, source_target_pairs={{4,0},{8,4},{12,8},{0,12},{5,1},{9,5},{13,9},{1,13},{6,2},{10,6},{... | collective-permute-start | bytes 6344 | tf_op jit(solution)/shard_map/ppermute | solution.py:17
  168.7 120.0 %all-reduce.10.cloned.1.call-start = ((), (), s32[]{:S(2)}) async-start(), calls=%async_computation.5 | async-start | bytes 131072 | tf_op jit(solution)/shard_map/psum | solution.py:39
  254.3 127.4 %all-reduce.12.cloned.1.call-start = ((), (), s32[]{:S(2)}) async-start(), calls=%async_computation.6 | async-start | bytes 131072 | tf_op jit(solution)/shard_map/psum | solution.py:39
  295.1 7.5 %collective-permute-start.23 = (f32[8,66,1]{2,1,0:T(8,128)S(1)}, f32[8,66,1]{2,1,0:T(8,128)S(1)}, u32[]{:S(2)}, u32[]{:S(2)}) collective-permute-start(f32[8,66,1]{2,1,0:T(8,128)S(1)} %get-tuple-element.9), channel_id=1, source_target_pairs={{0,4},{4,8},{8,12},{12,0},{1,5},{5,9},{9,13},{13,1},{2,6},{6,10},{... | collective-permute-start | bytes 6344 | tf_op jit(solution)/shard_map/ppermute | solution.py:16
  295.1 8.3 %collective-permute-start.22 = (f32[8,66,1]{2,1,0:T(8,128)S(1)}, f32[8,66,1]{2,1,0:T(8,128)S(1)}, u32[]{:S(2)}, u32[]{:S(2)}) collective-permute-start(f32[8,66,1]{2,1,0:T(8,128)S(1)} %get-tuple-element.8), channel_id=1, source_target_pairs={{4,0},{8,4},{12,8},{0,12},{5,1},{9,5},{13,9},{1,13},{6,2},{10,6},{... | collective-permute-start | bytes 6344 | tf_op jit(solution)/shard_map/ppermute | solution.py:17
  308.5 7.3 %collective-permute-start.27 = (f32[8,66,1]{2,1,0:T(8,128)S(1)}, f32[8,66,1]{2,1,0:T(8,128)S(1)}, u32[]{:S(2)}, u32[]{:S(2)}) collective-permute-start(f32[8,66,1]{2,1,0:T(8,128)S(1)} %get-tuple-element.7), channel_id=1, source_target_pairs={{0,4},{4,8},{8,12},{12,0},{1,5},{5,9},{9,13},{13,1},{2,6},{6,10},{... | collective-permute-start | bytes 6344 | tf_op jit(solution)/shard_map/ppermute | solution.py:16
  308.5 8.5 %collective-permute-start.26 = (f32[8,66,1]{2,1,0:T(8,128)S(1)}, f32[8,66,1]{2,1,0:T(8,128)S(1)}, u32[]{:S(2)}, u32[]{:S(2)}) collective-permute-start(f32[8,66,1]{2,1,0:T(8,128)S(1)} %get-tuple-element.6), channel_id=1, source_target_pairs={{4,0},{8,4},{12,8},{0,12},{5,1},{9,5},{13,9},{1,13},{6,2},{10,6},{... | collective-permute-start | bytes 6344 | tf_op jit(solution)/shard_map/ppermute | solution.py:17
  323.0 7.1 %collective-permute-start.31 = (f32[8,66,1]{2,1,0:T(8,128)S(1)}, f32[8,66,1]{2,1,0:T(8,128)S(1)}, u32[]{:S(2)}, u32[]{:S(2)}) collective-permute-start(f32[8,66,1]{2,1,0:T(8,128)S(1)} %get-tuple-element.5), channel_id=1, source_target_pairs={{0,4},{4,8},{8,12},{12,0},{1,5},{5,9},{9,13},{13,1},{2,6},{6,10},{... | collective-permute-start | bytes 6344 | tf_op jit(solution)/shard_map/ppermute | solution.py:16
  323.1 8.7 %collective-permute-start.30 = (f32[8,66,1]{2,1,0:T(8,128)S(1)}, f32[8,66,1]{2,1,0:T(8,128)S(1)}, u32[]{:S(2)}, u32[]{:S(2)}) collective-permute-start(f32[8,66,1]{2,1,0:T(8,128)S(1)} %get-tuple-element.4), channel_id=1, source_target_pairs={{4,0},{8,4},{12,8},{0,12},{5,1},{9,5},{13,9},{1,13},{6,2},{10,6},{... | collective-permute-start | bytes 6344 | tf_op jit(solution)/shard_map/ppermute | solution.py:17
  336.9 8.9 %collective-permute-start.34 = (f32[8,66,1]{2,1,0:T(8,128)S(1)}, f32[8,66,1]{2,1,0:T(8,128)S(1)}, u32[]{:S(2)}, u32[]{:S(2)}) collective-permute-start(f32[8,66,1]{2,1,0:T(8,128)S(1)} %get-tuple-element.2), channel_id=1, source_target_pairs={{4,0},{8,4},{12,8},{0,12},{5,1},{9,5},{13,9},{1,13},{6,2},{10,6},{... | collective-permute-start | bytes 6344 | tf_op jit(solution)/shard_map/ppermute | solution.py:17
  406.3 8.4 %all-to-all-start.2 = ((f32[1,8,512]{2,0,1:T(1,128)}), f32[1,8,512]{2,0,1:T(1,128)S(1)}, u32[]{:S(2)}, u32[]{:S(2)}) async-start(f32[1,8,512]{2,0,1:T(1,128)} %copy.14), calls=%async_computation.2 | async-start | bytes 32768 | tf_op jit(solution)/shard_map/all_to_all | solution.py:98
  (26 other events, 291.6 us)
Sparse Core Ops, SparseCore 0:
  76.4 34.0 all-reduce.5
  168.8 34.5 all-reduce.7
  254.5 34.2 all-reduce.9
  347.2 34.5 all-reduce.11
where the time goes:
time: 442 us
  waiting for transfers between devices  226 us (51%)
  local copies, waits for them, and re-layouts  86.3 us (20%)
  other arithmetic  69 us (16%)
  starting transfers between devices  46.3 us (10%)
  between operations  14.3 us (3%)
    psum x4, waiting for transfers between devices, member_total(): return lax.psum(partial_value, 'mem')  138 us
    ppermute x18, waiting for transfers between devices, extended(): before = lax.ppermute(last, axis, up)  53 us
    scatter-add x1, other arithmetic, per_device(): jax.ops.segment_sum(got_weight * at_obs, got_cell, num_segments=tile_cells)  26.3 us
    scatter-add x1, other arithmetic, per_device(): jax.ops.segment_sum(got_weight * got_depart, got_cell, num_segments=tile_...  26.3 us
    ppermute x18, waiting for transfers between devices, extended(): after = lax.ppermute(first, axis, down)  26.1 us
    ppermute x18, starting transfers between devices, extended(): after = lax.ppermute(first, axis, down)  24.6 us
    gather x2, local copies, waits for them, and re-layouts, per_device(): answer = got_depart - increment.reshape(-1)[got_cell]  23 us
    gather x1, local copies, waits for them, and re-layouts, per_device(): at_obs = first_pass.reshape(-1)[got_cell]  23 us
  transfers between devices with their start and end apart: 43, of which 40 were waited for; matrix products, arithmetic and copies ran while one was open for 2% of the time, Pallas kernels for 0%

commit v1 on v0

v1 whole, which is shorter than its diff:
```python
import functools

import jax
import jax.numpy as jnp
from jax import lax
from jax.experimental import pallas as pl
from jax.experimental.pallas import tpu as pltpu
from jax.sharding import PartitionSpec as P

STEPS = 4
LANES = 128
RIM = 8
F32 = jnp.float32
BF16 = jnp.bfloat16
MESH = pl.DeviceIdType.MESH
DIRECTIONS = [(0, 1), (0, -1), (1, 0), (-1, 0), (1, 1), (1, -1), (-1, 1), (-1, -1)]


def halves(value):
    high = value.astype(BF16).astype(F32)
    return high, value - high


def dot_nt(left, right):
    return lax.dot_general(left, right, (((1,), (1,)), ((), ())), preferred_element_type=F32)


def dot_nn(left, right):
    return lax.dot_general(left, right, (((1,), (0,)), ((), ())), preferred_element_type=F32)


def rows_iota(count):
    return lax.broadcasted_iota(jnp.int32, (count, LANES), 0)


def one_hot(index_row, count):
    return jnp.where(rows_iota(count) == index_row, 1.0, 0.0).astype(BF16)


def kernel(
    sizes,
    member_ref, rate_ref, sea_ref, owner_ref, cell_ref, depart_ref, weight_ref,
    increment_ref, residual_ref,
    member_ext, coef_ext, source1, source2, spread, member_all, north_all, east_all,
    outgoing, arrived, partial1, partial, gathered1, gathered2, gathered3, kept, answers, returned,
    rank_ref, total_ref, wide_ref,
    send_x, recv_x, send_c, recv_c, send_v1, recv_v1, send_v2, recv_v2, sums_sem, a2a_sem,
):
    lat_size, lon_size, mem_size, places, q, block_rows, divisor = sizes
    tile_rows, tile_cols = rate_ref.shape
    chunks = owner_ref.shape[0]
    lat = lax.axis_index("lat")
    lon = lax.axis_index("lon")
    mem = lax.axis_index("mem")
    place = lat * lon_size + lon
    quarter = tile_rows // mem_size
    shift_q = q.bit_length() - 1
    shift_b = block_rows.bit_length() - 1
    end = RIM + tile_rows
    ext_rows = tile_rows + 2 * RIM

    def place_at(step):
        other = lax.rem(place + step, places)
        return other, (other // lon_size, lax.rem(other, lon_size), mem)

    barrier = pltpu.get_barrier_semaphore()

    def greet(step, carry):
        pl.semaphore_signal(barrier, inc=1, device_id=place_at(step)[1], device_id_type=MESH)
        return carry

    lax.fori_loop(1, places, greet, 0)
    for step in range(1, mem_size):
        pl.semaphore_signal(
            barrier, inc=1, device_id=(lat, lon, lax.rem(mem + step, mem_size)), device_id_type=MESH
        )

    zero_rows = jnp.zeros((RIM, 512), F32)
    for ext in (source1, source2, coef_ext.at[0], coef_ext.at[1]):
        @pl.when(lat == 0)
        def _(ext=ext):
            ext[0:RIM, :] = zero_rows

        @pl.when(lat == lat_size - 1)
        def _(ext=ext):
            ext[end:ext_rows, :] = zero_rows

    @pl.when(lat == 0)
    def _():
        member_ext[0:RIM] = jnp.zeros((RIM, 8, 512), F32)

    @pl.when(lat == lat_size - 1)
    def _():
        member_ext[end:ext_rows] = jnp.zeros((RIM, 8, 512), F32)

    member_ext[RIM:end, :, 0:tile_cols] = member_ref[...]
    coef_ext[0, RIM:end, 0:tile_cols] = rate_ref[...]
    coef_ext[1, RIM:end, 0:tile_cols] = sea_ref[...].astype(F32)

    pl.semaphore_wait(barrier, places - 1 + mem_size - 1)

    def halo_copies(at, send_sem, recv_sem):
        made = []
        for k, (dy, dx) in enumerate(DIRECTIONS):
            source_rows = {0: pl.ds(RIM, tile_rows), 1: pl.ds(end - RIM, RIM), -1: pl.ds(RIM, RIM)}[dy]
            target_rows = {0: pl.ds(RIM, tile_rows), 1: pl.ds(0, RIM), -1: pl.ds(end, RIM)}[dy]
            source_cols = {0: pl.ds(0, 256), 1: pl.ds(128, 128), -1: pl.ds(0, 128)}[dx]
            target_cols = {0: pl.ds(0, 256), 1: pl.ds(384, 128), -1: pl.ds(256, 128)}[dx]
            copy = pltpu.make_async_remote_copy(
                src_ref=at(source_rows, source_cols),
                dst_ref=at(target_rows, target_cols),
                send_sem=send_sem.at[k],
                recv_sem=recv_sem.at[k],
                device_id=(lat + dy, lax.rem(lon + dx + lon_size, lon_size), mem),
                device_id_type=MESH,
            )
            sends = {0: None, 1: lat < lat_size - 1, -1: lat > 0}[dy]
            gets = {0: None, 1: lat > 0, -1: lat < lat_size - 1}[dy]
            made.append((copy, sends, gets))
        return made

    def when(condition, action):
        if condition is None:
            action()
        else:
            pl.when(condition)(action)

    def halo_start(copies):
        for copy, sends, gets in copies:
            when(sends, lambda copy=copy: copy.start())

    def halo_wait(copies):
        for copy, sends, gets in copies:
            when(sends, lambda copy=copy: copy.wait_send())
            when(gets, lambda copy=copy: copy.wait_recv())

    coef_copies = halo_copies(lambda r, c: coef_ext.at[:, r, c], send_c, recv_c)
    member_copies = halo_copies(lambda r, c: member_ext.at[r, :, c], send_x, recv_x)
    source_copies = [
        halo_copies(lambda r, c: source1.at[r, c], send_v1, recv_v1),
        halo_copies(lambda r, c: source2.at[r, c], send_v2, recv_v2),
    ]

    owner = owner_ref[...]
    upper = jnp.where(
        lax.broadcasted_iota(jnp.int32, (LANES, LANES), 0)
        < lax.broadcasted_iota(jnp.int32, (LANES, LANES), 1), 1.0, 0.0,
    ).astype(BF16)
    table = jnp.concatenate([upper, jnp.ones((LANES, LANES), BF16)], axis=1)
    before = jnp.zeros((places, LANES), F32)
    for r in range(chunks):
        match = one_hot(owner[r : r + 1], places)
        counts = dot_nn(match, table)
        found = jnp.sum(match.astype(F32) * (counts[:, :LANES] + before), axis=0, keepdims=True)
        rank_ref[r : r + 1, :] = found.astype(jnp.int32)
        before = before + counts[:, LANES:]
    rank = rank_ref[...]
    slot_row = owner * block_rows + lax.shift_right_logical(rank, 7)
    slot_lane = lax.bitwise_and(rank, 127)

    depart = depart_ref[...]
    weight = weight_ref[...]
    cell = cell_ref[...]
    product1, product2 = halves(weight * depart)
    weight1, weight2 = halves(weight)
    cell2 = lax.bitwise_and(cell, 127)
    cell1 = (cell - cell2).astype(F32)
    cell2 = cell2.astype(F32)
    pack_rows = places * block_rows
    row = rows_iota(pack_rows)
    inner = lax.bitwise_and(row, block_rows - 1)
    field = lax.shift_right_logical(inner, shift_q)
    base_row = row - lax.shift_left(field, shift_q)
    packed = jnp.zeros((pack_rows, LANES), F32)
    for r in range(0, chunks, 2):
        lefts1, lefts2, rights = [], [], []
        for c in (r, r + 1):
            s = slice(c, c + 1)
            hit = base_row == slot_row[s]
            lefts1.append(jnp.where(hit, jnp.where(field == 0, product1[s], jnp.where(field == 1, weight1[s], jnp.where(field == 2, cell1[s], 0.0))), 0.0).astype(BF16))
            lefts2.append(jnp.where(hit, jnp.where(field == 0, product2[s], jnp.where(field == 1, weight2[s], jnp.where(field == 2, cell2[s], 0.0))), 0.0).astype(BF16))
            rights.append(one_hot(slot_lane[s], LANES))
        right = jnp.concatenate(rights, axis=1)
        packed = packed + dot_nt(jnp.concatenate(lefts1, axis=1), right)
        packed = packed + dot_nt(jnp.concatenate(lefts2, axis=1), right)
    outgoing[...] = packed.reshape(places, block_rows, LANES)

    def exchange(from_ref, to_ref, sems):
        def send(step, carry):
            other, device = place_at(step)
            pltpu.make_async_remote_copy(
                src_ref=from_ref.at[other], dst_ref=to_ref.at[place],
                send_sem=sems.at[0], recv_sem=sems.at[1],
                device_id=device, device_id_type=MESH,
            ).start()
            return carry

        lax.fori_loop(1, places, send, 0)

    def exchange_wait(from_ref, to_ref, sems):
        whole = pltpu.make_async_remote_copy(
            src_ref=from_ref.at[pl.ds(0, places - 1)], dst_ref=to_ref.at[pl.ds(0, places - 1)],
            send_sem=sems.at[0], recv_sem=sems.at[1],
            device_id=place_at(1)[1], device_id_type=MESH,
        )
        whole.wait_send()
        whole.wait_recv()

    exchange(outgoing, arrived, a2a_sem.at[0])
    halo_start(coef_copies)
    halo_start(member_copies)
    arrived[place] = outgoing[place]
    exchange_wait(outgoing, arrived, a2a_sem.at[0])

    def slot_cells(block):
        whole = block[2 * q : 3 * q].astype(jnp.int32)
        lane = lax.bitwise_and(whole, 127)
        half = lax.bitwise_and(lax.shift_right_logical(whole, 7), 1)
        return lax.shift_right_logical(whole, 8) + half * tile_rows, lane

    halves_rows = 2 * tile_rows
    total_ref[...] = jnp.zeros_like(total_ref)

    def add_block(origin, carry):
        block = arrived[origin]
        high, lane = slot_cells(block)
        lefts, rights = [], []
        for k in range(q):
            hit = rows_iota(halves_rows) == high[k : k + 1]
            parts = halves(block[k : k + 1]) + halves(block[q + k : q + k + 1])
            lefts.append(jnp.concatenate([jnp.where(hit, part, 0.0).astype(BF16) for part in parts], axis=0))
            rights.append(one_hot(lane[k : k + 1], LANES))
        total_ref[...] += dot_nt(jnp.concatenate(lefts, axis=1), jnp.concatenate(rights, axis=1))
        return carry

    lax.fori_loop(0, places, add_block, 0)
    h = halves_rows
    for f in range(2):
        both = total_ref[2 * f * h : (2 * f + 1) * h, :] + total_ref[(2 * f + 1) * h : (2 * f + 2) * h, :]
        partial1[f, :, 0:LANES] = both[:tile_rows]
        partial1[f, :, LANES : 2 * LANES] = both[tile_rows:]

    my_rows = pl.multiple_of(mem * quarter, quarter)

    def member_sum(part_at, got, number):
        sems = sums_sem.at[2 * number]
        for step in range(1, mem_size):
            other = lax.rem(mem + step, mem_size)
            pltpu.make_async_remote_copy(
                src_ref=part_at(pl.ds(pl.multiple_of(other * quarter, quarter), quarter)),
                dst_ref=got.at[mem],
                send_sem=sems.at[0], recv_sem=sems.at[1],
                device_id=(lat, lon, other), device_id_type=MESH,
            ).start()
        got[mem] = part_at(pl.ds(my_rows, quarter))[...]
        whole = pltpu.make_async_remote_copy(
            src_ref=got.at[pl.ds(0, mem_size - 1)], dst_ref=got.at[pl.ds(0, mem_size - 1)],
            send_sem=sems.at[0], recv_sem=sems.at[1],
            device_id=(lat, lon, lax.rem(mem + 1, mem_size)), device_id_type=MESH,
        )
        whole.wait_send()
        whole.wait_recv()
        total = got[0]
        for other in range(1, mem_size):
            total = total + got[other]
        return total

    def member_share(ref, first, number):
        sems = sums_sem.at[2 * number + 1]
        mine = ref.at[pl.ds(first + my_rows, quarter), pl.ds(0, tile_cols)]
        for step in range(1, mem_size):
            pltpu.make_async_remote_copy(
                src_ref=mine, dst_ref=mine,
                send_sem=sems.at[0], recv_sem=sems.at[1],
                device_id=(lat, lon, lax.rem(mem + step, mem_size)), device_id_type=MESH,
            ).start()
        rest = ref.at[pl.ds(first, (mem_size - 1) * quarter), pl.ds(0, tile_cols)]
        whole = pltpu.make_async_remote_copy(
            src_ref=rest, dst_ref=rest, send_sem=sems.at[0], recv_sem=sems.at[1],
            device_id=(lat, lon, lax.rem(mem + 1, mem_size)), device_id_type=MESH,
        )
        whole.wait_send()
        whole.wait_recv()

    summed = member_sum(lambda rows: partial1.at[:, rows], gathered1, 0)
    kept[...] = summed
    source1[pl.ds(RIM + my_rows, quarter), 0:tile_cols] = summed[0]
    member_share(source1, RIM, 0)
    halo_start(source_copies[0])

    lane = lax.broadcasted_iota(jnp.int32, (1, LANES), 1)

    def joined(value):
        side = jnp.where(lane < 64, value[..., 256:384], value[..., 384:512])
        return jnp.concatenate([value[..., 0:256], side], axis=-1)

    halo_wait(coef_copies)
    halo_wait(member_copies)
    rate = joined(coef_ext[0])
    sea = joined(coef_ext[1])
    below = lambda a: jnp.concatenate([a[1:], a[:1]], axis=0)
    width = 384
    wide_ref[0] = 0.5 * (rate + below(rate)) * sea * below(sea)
    wide_ref[1] = 0.5 * (rate + pltpu.roll(rate, width - 1, 1)) * sea * pltpu.roll(sea, width - 1, 1)

    def widen(step, carry):
        base = pl.multiple_of(step * 8, 8)
        for u in range(8):
            i = base + u
            north_all[i] = jnp.broadcast_to(wide_ref[0, pl.ds(i, 1), :], (8, width))
            east_all[i] = jnp.broadcast_to(wide_ref[1, pl.ds(i, 1), :], (8, width))
            value = member_ext[i]
            side = jnp.where(lane < 64, value[:, 256:384], value[:, 384:512])
            member_all[i, :, 0:256] = value[:, 0:256]
            member_all[i, :, 256:384] = side
        return carry

    lax.fori_loop(0, ext_rows // 8, widen, 0)

    def covariance(source):
        wide_ref[0] = joined(source[...])

        def sweep(read, write):
            at = read(3)
            here = read(4)

            def rows(step, carry):
                here, flux = carry
                for u in range(8):
                    i = 4 + step * 8 + u
                    after = read(i + 1)
                    flux_after = north_all[i] * (after - here)
                    flux_east = east_all[i] * (pltpu.roll(here, width - 1, 1) - here)
                    write(i, here + (flux_after - flux) + (flux_east - pltpu.roll(flux_east, 1, 1)))
                    here, flux = after, flux_after
                return here, flux

            lax.fori_loop(0, (tile_rows + 8) // 8, rows, (here, north_all[3] * (here - at)))

        def begin(i):
            return member_all[i] * wide_ref[0, pl.ds(i, 1), :]

        def keep(i, value):
            spread[i] = value

        spread[3] = begin(3)
        spread[tile_rows + 12] = begin(tile_rows + 12)
        sweep(begin, keep)
        for turn in range(STEPS - 1):
            sweep(lambda i: spread[i], keep)

        def collect(step, carry):
            base = pl.multiple_of(step * 8, 8)
            found = [
                jnp.sum(spread[RIM + base + u, :, 0:256] * member_all[RIM + base + u, :, 0:256], axis=0, keepdims=True)
                for u in range(8)
            ]
            partial[pl.ds(base, 8), :] = jnp.concatenate(found, axis=0)
            return carry

        lax.fori_loop(0, tile_rows // 8, collect, 0)

    my_sea = lambda: coef_ext[1, pl.ds(RIM + my_rows, quarter), 0:tile_cols]
    halo_wait(source_copies[0])
    covariance(source1)
    first_pass = my_sea() * member_sum(lambda rows: partial.at[rows], gathered2, 1) / divisor
    source2[pl.ds(RIM + my_rows, quarter), 0:tile_cols] = kept[0] - kept[1] * first_pass
    member_share(source2, RIM, 1)
    halo_start(source_copies[1])
    halo_wait(source_copies[1])
    covariance(source2)
    wide = my_sea() * member_sum(lambda rows: partial.at[rows], gathered3, 2) / divisor
    increment_ref[pl.ds(my_rows, quarter), :] = wide
    member_share(increment_ref, 0, 2)

    field_value = increment_ref[...]
    stacked = jnp.concatenate([field_value[:, :LANES], field_value[:, LANES:]], axis=0)
    first, second = halves(stacked)
    lookup = jnp.concatenate([first, second], axis=0).astype(BF16)

    def look(origin, carry):
        high, lane_of = slot_cells(arrived[origin])
        found = []
        for k in range(q):
            got = dot_nn(lookup, one_hot(lane_of[k : k + 1], LANES))
            value = got[:halves_rows] + got[halves_rows:]
            hit = rows_iota(halves_rows) == high[k : k + 1]
            found.append(jnp.sum(jnp.where(hit, value, 0.0), axis=0, keepdims=True))
        found.append(jnp.zeros((8 - q, LANES), F32))
        answers[origin] = jnp.concatenate(found, axis=0)
        return carry

    lax.fori_loop(0, places, look, 0)
    exchange(answers, returned, a2a_sem.at[1])
    returned[place] = answers[place]
    exchange_wait(answers, returned, a2a_sem.at[1])
    first, second = halves(returned[...].reshape(places * 8, LANES))
    lookup = jnp.concatenate([first, second], axis=0).astype(BF16)
    answer_row = owner * 8 + lax.shift_right_logical(rank_ref[...], 7)
    answer_lane = lax.bitwise_and(rank_ref[...], 127)
    for r in range(chunks):
        got = dot_nn(lookup, one_hot(answer_lane[r : r + 1], LANES))
        value = got[: places * 8] + got[places * 8 :]
        hit = rows_iota(places * 8) == answer_row[r : r + 1]
        found = jnp.sum(jnp.where(hit, value, 0.0), axis=0, keepdims=True)
        residual_ref[r : r + 1, :] = depart_ref[r : r + 1, :] - found


def per_device(sizes, perturbations, diffusivity, sea_mask, obs_owner, obs_cell, obs_depart, obs_weight):
    lat_size, lon_size, mem_size = sizes
    members, tile_rows, tile_cols = perturbations.shape
    count = obs_cell.shape[0]
    places = lat_size * lon_size
    capacity = max(2, 2 * count // places)
    q = max(1, capacity // LANES)
    block_rows = 8
    while block_rows < 3 * q:
        block_rows *= 2
    rows = count // LANES
    ext = tile_rows + 2 * RIM
    quarter = tile_rows // mem_size
    divisor = members * mem_size - 1
    vmem = pltpu.VMEM
    dma = pltpu.SemaphoreType.DMA
    as_rows = lambda a: a.reshape(rows, LANES)
    member_rows = jnp.transpose(perturbations, (1, 0, 2)).astype(F32)
    increment, residual = pl.pallas_call(
        functools.partial(kernel, (lat_size, lon_size, mem_size, places, q, block_rows, divisor)),
        out_shape=(
            jax.ShapeDtypeStruct((tile_rows, tile_cols), F32),
            jax.ShapeDtypeStruct((rows, LANES), F32),
        ),
        in_specs=[pl.BlockSpec(memory_space=vmem)] * 7,
        out_specs=(pl.BlockSpec(memory_space=vmem),) * 2,
        scratch_shapes=[
            vmem((ext, 8, 512), F32),
            vmem((2, ext, 512), F32),
            vmem((ext, 512), F32),
            vmem((ext, 512), F32),
            vmem((ext, 8, 384), F32),
            vmem((ext, 8, 384), F32),
            vmem((ext, 8, 384), F32),
            vmem((ext, 8, 384), F32),
            vmem((places, block_rows, LANES), F32),
            vmem((places, block_rows, LANES), F32),
            vmem((2, tile_rows, tile_cols), F32),
            vmem((tile_rows, tile_cols), F32),
            vmem((mem_size, 2, quarter, tile_cols), F32),
            vmem((mem_size, quarter, tile_cols), F32),
            vmem((mem_size, quarter, tile_cols), F32),
            vmem((2, quarter, tile_cols), F32),
            vmem((places, 8, LANES), F32),
            vmem((places, 8, LANES), F32),
            vmem((rows, LANES), jnp.int32),
            vmem((8 * tile_rows, LANES), F32),
            vmem((2, ext, 384), F32),
        ] + [dma((8,))] * 8 + [dma((6, 2)), dma((2, 2))],
        compiler_params=pltpu.CompilerParams(
            collective_id=0, has_side_effects=True, vmem_limit_bytes=40 * 1024 * 1024
        ),
        name="update",
    )(
        member_rows, diffusivity, sea_mask,
        as_rows(obs_owner), as_rows(obs_cell), as_rows(obs_depart), as_rows(obs_weight),
    )
    return increment, residual.reshape(count)


def solution(mesh):
    sizes = tuple(mesh.shape[name] for name in ("lat", "lon", "mem"))
    return jax.shard_map(
        functools.partial(per_device, sizes),
        mesh=mesh,
        in_specs=(
            P("mem", "lat", "lon"),
            P("lat", "lon"),
            P("lat", "lon"),
            P(("lat", "lon", "mem"), None),
            P(("lat", "lon", "mem")),
            P(("lat", "lon", "mem")),
            P(("lat", "lon", "mem")),
        ),
        out_specs=(P("lat", "lon"), P(("lat", "lon", "mem"))),
        check_vma=False,
    )
```

time: 442 us -> 64.1 us (0.15)
  waiting for transfers between devices: 226 us -> 0 us
  local copies, waits for them, and re-layouts: 86.3 us -> 1.26 us
  other arithmetic: 69 us -> 1.17 us
  Pallas kernels: 0 us -> 60.8 us
  starting transfers between devices: 46.3 us -> 0 us
  between operations: 14.3 us -> 0.74 us
    psum x4 -> x0, waiting for transfers between devices: 138 us -> none  [member_total(): return lax.psum(partial_value, 'mem')]
    ppermute x36 -> x0, waiting for transfers between devices: 79.1 us -> none  [the longest x18 53 us: extended(): before = lax.ppermute(last, axis, up)]
    gather x4 -> x0, local copies, waits for them, and re-layouts: 66.6 us -> none  [the longest x2 23 us: per_device(): answer = got_depart - increment.reshape(-1)[got_cell]]
    pallas_call x0 -> x1, Pallas kernels: none -> 60.8 us  [per_device(): pl.pallas_call(functools.partial(kernel, (lat_size, lon_size, mem_size, p...]
    scatter-add x2 -> x0, other arithmetic: 52.5 us -> none  [the longest x1 26.3 us: per_device(): jax.ops.segment_sum(got_weight * at_obs, got_cell, num_segments=tile_cells)]
    ppermute x36 -> x0, starting transfers between devices: 33.7 us -> none  [the longest x18 24.6 us: extended(): after = lax.ppermute(first, axis, down)]
    all_to_all x3 -> x0, starting transfers between devices: 12.2 us -> none  [the longest x1 5.17 us: per_device(): lax.all_to_all(outgoing, ('lat', 'lon'), split_axis=1, concat_axis=1, til...]
    all_to_all x3 -> x0, waiting for transfers between devices: 9.25 us -> none  [the longest x1 4.7 us: per_device(): lax.all_to_all(answer[None], ('lat', 'lon'), split_axis=1, concat_axis=1,...]
  transfers between devices with their start and end apart: 43 -> 0, of which waited for: 40 -> 0; matrix products, arithmetic and copies ran while one was open for 2% -> 0% of each run, Pallas kernels for 0% -> 0%
where the time goes in v1:
time: 64.1 us; the launch traced here: 63.9 us
  Pallas kernels  60.8 us (95%)
  local copies, waits for them, and re-layouts  1.26 us (2%)
  other arithmetic  1.17 us (2%)
  between operations  0.74 us (1%)
    pallas_call x1, Pallas kernels, per_device(): pl.pallas_call(functools.partial(kernel, (lat_size, lon_size, mem_size, p...  60.8 us

profile of v1, /device:TPU:0, one launch (start us, length us, event | category | flops | bytes accessed | tf_op | source)
XLA Modules:
  0.0 63.9 jit_solution(1701588957430891698)
XLA Ops:
  0.6 0.0 copy-start
  0.6 0.0 copy-start.1
  0.7 0.0 copy-start.2
  0.7 0.0 copy-start.3
  0.7 0.0 copy-start.4
  0.7 0.0 copy-start.5
  0.7 1.2 %convert_bitcast_fusion.member_ref = f32[64,8,256]{2,1,0:T(8,128)S(1)} fusion(bf16[8,64,256]{2,1,0:T(8,128)(2,1)} %param.7), kind=kLoop, calls=%fused_computation | loop fusion | flops 131072 | bytes 786432 | tf_op jit(solution)/shard_map/convert_element_type | solution.py:426
  1.9 0.0 copy-done
  1.9 0.0 copy-done.1
  1.9 0.0 copy-done.2
  1.9 0.0 copy-done.3
  1.9 0.0 copy-done.4
  1.9 0.0 copy-done.5
  1.9 60.8 %update.1 = (f32[64,256]{1,0:T(8,128)S(1)}, f32[16,128]{1,0:T(8,128)S(1)}) custom-call(f32[64,8,256]{2,1,0:T(8,128)S(1)} %convert_bitcast_fusion.member_ref, f32[64,256]{1,0:T(8,128)S(1)} %copy-done, s32[64,256]{1,0:T(8,128)S(1)} %copy-done.1, s32[16,128]{1,0:T(8,128)S(1)} %bitcast.7, s32[16,128]{1,0:T(8,128)S(1)} %bitcast.8, f32[16,128]{1,0:T(8,128)S(1)} %bitcast.9, ...), custom_call_target="tpu_custom_call" | custom-call | tf_op jit(solution)/shard_map/update/pallas_call | solution.py:427
  62.7 0.6 copy.13
  63.3 0.6 copy.14
Async XLA Ops:
  0.6 1.2 %copy-start = (f32[64,256]{1,0:T(8,128)S(1)}, f32[64,256]{1,0:T(8,128)}, u32[]{:S(2)}) copy-start(f32[64,256]{1,0:T(8,128)} %rate_ref.1) | copy-start | bytes 196612
  0.6 1.2 %copy-start.1 = (s32[64,256]{1,0:T(8,128)S(1)}, s32[64,256]{1,0:T(8,128)}, u32[]{:S(2)}) copy-start(s32[64,256]{1,0:T(8,128)} %sea_ref.1) | copy-start | bytes 196612
  0.7 1.2 %copy-start.2 = (s32[2048,1]{0,1:T(1,128)S(1)}, s32[2048,1]{0,1:T(1,128)}, u32[]{:S(2)}) copy-start(s32[2048,1]{0,1:T(1,128)} %param.10) | copy-start | bytes 24580
  0.7 1.2 %copy-start.3 = (s32[2048]{0:T(1024)S(1)}, s32[2048]{0:T(1024)}, u32[]{:S(2)}) copy-start(s32[2048]{0:T(1024)} %param.11) | copy-start | bytes 24580
  0.7 1.2 %copy-start.4 = (f32[2048]{0:T(1024)S(1)}, f32[2048]{0:T(1024)}, u32[]{:S(2)}) copy-start(f32[2048]{0:T(1024)} %param.12) | copy-start | bytes 24580
  0.7 1.2 %copy-start.5 = (f32[2048]{0:T(1024)S(1)}, f32[2048]{0:T(1024)}, u32[]{:S(2)}) copy-start(f32[2048]{0:T(1024)} %param.13) | copy-start | bytes 24580

commit v2 on v1

--- a/solution.py
+++ b/solution.py
@@ -242,16 +242,22 @@
 
     my_rows = pl.multiple_of(mem * quarter, quarter)
 
+    def sum_copy(part_at, got, number, other):
+        sems = sums_sem.at[2 * number]
+        return pltpu.make_async_remote_copy(
+            src_ref=part_at(pl.ds(pl.multiple_of(other * quarter, quarter), quarter)),
+            dst_ref=got.at[mem],
+            send_sem=sems.at[0], recv_sem=sems.at[1],
+            device_id=(lat, lon, other), device_id_type=MESH,
+        )
+
+    def sum_part(part_at, got, number, other):
+        @pl.when(mem != other)
+        def _():
+            sum_copy(part_at, got, number, other).start()
+
     def member_sum(part_at, got, number):
         sems = sums_sem.at[2 * number]
-        for step in range(1, mem_size):
-            other = lax.rem(mem + step, mem_size)
-            pltpu.make_async_remote_copy(
-                src_ref=part_at(pl.ds(pl.multiple_of(other * quarter, quarter), quarter)),
-                dst_ref=got.at[mem],
-                send_sem=sems.at[0], recv_sem=sems.at[1],
-                device_id=(lat, lon, other), device_id_type=MESH,
-            ).start()
         got[mem] = part_at(pl.ds(my_rows, quarter))[...]
         whole = pltpu.make_async_remote_copy(
             src_ref=got.at[pl.ds(0, mem_size - 1)], dst_ref=got.at[pl.ds(0, mem_size - 1)],
@@ -282,7 +288,10 @@
         whole.wait_send()
         whole.wait_recv()
 
-    summed = member_sum(lambda rows: partial1.at[:, rows], gathered1, 0)
+    first_part = lambda rows: partial1.at[:, rows]
+    for step in range(1, mem_size):
+        sum_copy(first_part, gathered1, 0, lax.rem(mem + step, mem_size)).start()
+    summed = member_sum(first_part, gathered1, 0)
     kept[...] = summed
     source1[pl.ds(RIM + my_rows, quarter), 0:tile_cols] = summed[0]
     member_share(source1, RIM, 0)
@@ -317,59 +326,74 @@
 
     lax.fori_loop(0, ext_rows // 8, widen, 0)
 
-    def covariance(source):
+    def covariance(source, finished):
         wide_ref[0] = joined(source[...])
 
-        def sweep(read, write):
-            at = read(3)
-            here = read(4)
-
+        def step_rows(read, base, carry, count):
+            here, flux = carry
+            values = [here] + [read(base + u + 1) for u in range(count)]
+            results = []
+            for u in range(count):
+                here, after = values[u], values[u + 1]
+                flux_after = north_all[base + u] * (after - here)
+                flux_east = east_all[base + u] * (pltpu.roll(here, width - 1, 1) - here)
+                results.append(here + (flux_after - flux) + (flux_east - pltpu.roll(flux_east, 1, 1)))
+                flux = flux_after
+            return results, (values[-1], flux)
+
+        def first_of(read, row):
+            here = read(row)
+            return here, north_all[row - 1] * (here - read(row - 1))
+
+        def sweep(read):
             def rows(step, carry):
-                here, flux = carry
+                base = 4 + step * 8
+                results, carry = step_rows(read, base, carry, 8)
                 for u in range(8):
-                    i = 4 + step * 8 + u
-                    after = read(i + 1)
-                    flux_after = north_all[i] * (after - here)
-                    flux_east = east_all[i] * (pltpu.roll(here, width - 1, 1) - here)
-                    write(i, here + (flux_after - flux) + (flux_east - pltpu.roll(flux_east, 1, 1)))
-                    here, flux = after, flux_after
-                return here, flux
-
-            lax.fori_loop(0, (tile_rows + 8) // 8, rows, (here, north_all[3] * (here - at)))
+                    spread[base + u] = results[u]
+                return carry
+
+            lax.fori_loop(0, (tile_rows + 8) // 8, rows, first_of(read, 4))
 
         def begin(i):
             return member_all[i] * wide_ref[0, pl.ds(i, 1), :]
 
-        def keep(i, value):
-            spread[i] = value
+        def again(i):
+            return spread[i]
 
         spread[3] = begin(3)
         spread[tile_rows + 12] = begin(tile_rows + 12)
-        sweep(begin, keep)
-        for turn in range(STEPS - 1):
-            sweep(lambda i: spread[i], keep)
-
-        def collect(step, carry):
-            base = pl.multiple_of(step * 8, 8)
+        sweep(begin)
+        for turn in range(STEPS - 2):
+            sweep(again)
+
+        def last_rows(step, carry):
+            base = RIM + step * 8
+            results, carry = step_rows(again, base, carry, 8)
             found = [
-                jnp.sum(spread[RIM + base + u, :, 0:256] * member_all[RIM + base + u, :, 0:256], axis=0, keepdims=True)
+                jnp.sum(results[u][:, 0:256] * member_all[base + u, :, 0:256], axis=0, keepdims=True)
                 for u in range(8)
             ]
-            partial[pl.ds(base, 8), :] = jnp.concatenate(found, axis=0)
+            partial[pl.ds(pl.multiple_of(step * 8, 8), 8), :] = jnp.concatenate(found, axis=0)
             return carry
 
-        lax.fori_loop(0, tile_rows // 8, collect, 0)
+        carry = first_of(again, RIM)
+        steps = quarter // 8
+        for part in range(mem_size):
+            carry = lax.fori_loop(part * steps, (part + 1) * steps, last_rows, carry)
+            finished(part)
 
     my_sea = lambda: coef_ext[1, pl.ds(RIM + my_rows, quarter), 0:tile_cols]
     halo_wait(source_copies[0])
-    covariance(source1)
-    first_pass = my_sea() * member_sum(lambda rows: partial.at[rows], gathered2, 1) / divisor
+    later_part = lambda rows: partial.at[rows]
+    covariance(source1, lambda part: sum_part(later_part, gathered2, 1, part))
+    first_pass = my_sea() * member_sum(later_part, gathered2, 1) / divisor
     source2[pl.ds(RIM + my_rows, quarter), 0:tile_cols] = kept[0] - kept[1] * first_pass
     member_share(source2, RIM, 1)
     halo_start(source_copies[1])
     halo_wait(source_copies[1])
-    covariance(source2)
-    wide = my_sea() * member_sum(lambda rows: partial.at[rows], gathered3, 2) / divisor
+    covariance(source2, lambda part: sum_part(later_part, gathered3, 2, part))
+    wide = my_sea() * member_sum(later_part, gathered3, 2) / divisor
     increment_ref[pl.ds(my_rows, quarter), :] = wide
     member_share(increment_ref, 0, 2)
 

time: 64.1 us -> 62.3 us (0.972)
  Pallas kernels: 60.8 us -> 59 us
    pallas_call x1, Pallas kernels: 60.8 us -> 59 us  [per_device(): pl.pallas_call(functools.partial(kernel, (lat_size, lon_size, mem_size, p...]
where the time goes in v2:
time: 62.3 us; the launch traced here: 62.2 us
  Pallas kernels  59 us (95%)
  local copies, waits for them, and re-layouts  1.26 us (2%)
  other arithmetic  1.17 us (2%)
  between operations  0.74 us (1%)
    pallas_call x1, Pallas kernels, per_device(): pl.pallas_call(functools.partial(kernel, (lat_size, lon_size, mem_size, p...  59 us
    unnamed x14, local copies, waits for them, and re-layouts  1.26 us

profile of v2, /device:TPU:0, one launch (start us, length us, event | category | flops | bytes accessed | tf_op | source)
XLA Modules:
  0.0 62.2 jit_solution(10085126019645444626)
XLA Ops:
  0.6 0.0 copy-start
  0.6 0.0 copy-start.1
  0.7 0.0 copy-start.2
  0.7 0.0 copy-start.3
  0.7 0.0 copy-start.4
  0.7 0.0 copy-start.5
  0.7 1.2 %convert_bitcast_fusion.member_ref = f32[64,8,256]{2,1,0:T(8,128)S(1)} fusion(bf16[8,64,256]{2,1,0:T(8,128)(2,1)} %param.7), kind=kLoop, calls=%fused_computation | loop fusion | flops 131072 | bytes 786432 | tf_op jit(solution)/shard_map/convert_element_type | solution.py:450
  1.9 0.0 copy-done
  1.9 0.0 copy-done.1
  1.9 0.0 copy-done.2
  1.9 0.0 copy-done.3
  1.9 0.0 copy-done.4
  1.9 0.0 copy-done.5
  1.9 59.0 %update.1 = (f32[64,256]{1,0:T(8,128)S(1)}, f32[16,128]{1,0:T(8,128)S(1)}) custom-call(f32[64,8,256]{2,1,0:T(8,128)S(1)} %convert_bitcast_fusion.member_ref, f32[64,256]{1,0:T(8,128)S(1)} %copy-done, s32[64,256]{1,0:T(8,128)S(1)} %copy-done.1, s32[16,128]{1,0:T(8,128)S(1)} %bitcast.7, s32[16,128]{1,0:T(8,128)S(1)} %bitcast.8, f32[16,128]{1,0:T(8,128)S(1)} %bitcast.9, ...), custom_call_target="tpu_custom_call" | custom-call | tf_op jit(solution)/shard_map/update/pallas_call | solution.py:451
  61.0 0.6 %copy.13 = f32[64,256]{1,0:T(8,128)} copy(f32[64,256]{1,0:T(8,128)S(1)} %get-tuple-element.8) | data formatting | bytes 131072
  61.6 0.6 copy.14
Async XLA Ops:
  0.6 1.2 %copy-start = (f32[64,256]{1,0:T(8,128)S(1)}, f32[64,256]{1,0:T(8,128)}, u32[]{:S(2)}) copy-start(f32[64,256]{1,0:T(8,128)} %rate_ref.1) | copy-start | bytes 196612
  0.6 1.2 %copy-start.1 = (s32[64,256]{1,0:T(8,128)S(1)}, s32[64,256]{1,0:T(8,128)}, u32[]{:S(2)}) copy-start(s32[64,256]{1,0:T(8,128)} %sea_ref.1) | copy-start | bytes 196612
  0.7 1.2 %copy-start.2 = (s32[2048,1]{0,1:T(1,128)S(1)}, s32[2048,1]{0,1:T(1,128)}, u32[]{:S(2)}) copy-start(s32[2048,1]{0,1:T(1,128)} %param.10) | copy-start | bytes 24580
  0.7 1.2 %copy-start.3 = (s32[2048]{0:T(1024)S(1)}, s32[2048]{0:T(1024)}, u32[]{:S(2)}) copy-start(s32[2048]{0:T(1024)} %param.11) | copy-start | bytes 24580
  0.7 1.2 %copy-start.4 = (f32[2048]{0:T(1024)S(1)}, f32[2048]{0:T(1024)}, u32[]{:S(2)}) copy-start(f32[2048]{0:T(1024)} %param.12) | copy-start | bytes 24580
  0.7 1.2 %copy-start.5 = (f32[2048]{0:T(1024)S(1)}, f32[2048]{0:T(1024)}, u32[]{:S(2)}) copy-start(f32[2048]{0:T(1024)} %param.13) | copy-start | bytes 24580

commit v3 on v2

--- a/solution.py
+++ b/solution.py
@@ -43,7 +43,7 @@
     increment_ref, residual_ref,
     member_ext, coef_ext, source1, source2, spread, member_all, north_all, east_all,
     outgoing, arrived, partial1, partial, gathered1, gathered2, gathered3, kept, answers, returned,
-    rank_ref, total_ref, wide_ref,
+    rank_ref, total_ref, wide_ref, lane_hot, column_hot,
     send_x, recv_x, send_c, recv_c, send_v1, recv_v1, send_v2, recv_v2, sums_sem, a2a_sem,
 ):
     lat_size, lon_size, mem_size, places, q, block_rows, divisor = sizes
@@ -148,12 +148,15 @@
     ).astype(BF16)
     table = jnp.concatenate([upper, jnp.ones((LANES, LANES), BF16)], axis=1)
     before = jnp.zeros((places, LANES), F32)
+    match = jnp.concatenate(
+        [jnp.where(rows_iota(places) == owner[r : r + 1], 1.0, 0.0) for r in range(chunks)], axis=0
+    )
+    counts = dot_nn(match.astype(BF16), table)
     for r in range(chunks):
-        match = one_hot(owner[r : r + 1], places)
-        counts = dot_nn(match, table)
-        found = jnp.sum(match.astype(F32) * (counts[:, :LANES] + before), axis=0, keepdims=True)
+        part = slice(r * places, (r + 1) * places)
+        found = jnp.sum(match[part] * (counts[part, :LANES] + before), axis=0, keepdims=True)
         rank_ref[r : r + 1, :] = found.astype(jnp.int32)
-        before = before + counts[:, LANES:]
+        before = before + counts[part, LANES:]
     rank = rank_ref[...]
     slot_row = owner * block_rows + lax.shift_right_logical(rank, 7)
     slot_lane = lax.bitwise_and(rank, 127)
@@ -171,18 +174,21 @@
     inner = lax.bitwise_and(row, block_rows - 1)
     field = lax.shift_right_logical(inner, shift_q)
     base_row = row - lax.shift_left(field, shift_q)
-    packed = jnp.zeros((pack_rows, LANES), F32)
-    for r in range(0, chunks, 2):
-        lefts1, lefts2, rights = [], [], []
-        for c in (r, r + 1):
+    packed = jnp.zeros((2 * pack_rows, LANES), F32)
+    for r in range(0, chunks, 4):
+        lefts = []
+        for c in range(r, r + 4):
             s = slice(c, c + 1)
             hit = base_row == slot_row[s]
-            lefts1.append(jnp.where(hit, jnp.where(field == 0, product1[s], jnp.where(field == 1, weight1[s], jnp.where(field == 2, cell1[s], 0.0))), 0.0).astype(BF16))
-            lefts2.append(jnp.where(hit, jnp.where(field == 0, product2[s], jnp.where(field == 1, weight2[s], jnp.where(field == 2, cell2[s], 0.0))), 0.0).astype(BF16))
-            rights.append(one_hot(slot_lane[s], LANES))
-        right = jnp.concatenate(rights, axis=1)
-        packed = packed + dot_nt(jnp.concatenate(lefts1, axis=1), right)
-        packed = packed + dot_nt(jnp.concatenate(lefts2, axis=1), right)
+            parts = [
+                jnp.where(field == 0, of_product[s], jnp.where(field == 1, of_weight[s], of_cell[s]))
+                for of_product, of_weight, of_cell in ((product1, weight1, cell1), (product2, weight2, cell2))
+            ]
+            lefts.append(jnp.concatenate([jnp.where(hit, p, 0.0) for p in parts], axis=0).astype(BF16))
+            lane_hot[:, c * LANES : (c + 1) * LANES] = one_hot(slot_lane[s], LANES)
+        right = lane_hot[:, r * LANES : (r + 4) * LANES]
+        packed = packed + dot_nt(jnp.concatenate(lefts, axis=1), right)
+    packed = packed[:pack_rows] + packed[pack_rows:]
     outgoing[...] = packed.reshape(places, block_rows, LANES)
 
     def exchange(from_ref, to_ref, sems):
@@ -214,31 +220,29 @@
 
     def slot_cells(block):
         whole = block[2 * q : 3 * q].astype(jnp.int32)
-        lane = lax.bitwise_and(whole, 127)
-        half = lax.bitwise_and(lax.shift_right_logical(whole, 7), 1)
-        return lax.shift_right_logical(whole, 8) + half * tile_rows, lane
-
-    halves_rows = 2 * tile_rows
+        return lax.shift_right_logical(whole, 8), lax.bitwise_and(whole, 255)
+
     total_ref[...] = jnp.zeros_like(total_ref)
-
-    def add_block(origin, carry):
-        block = arrived[origin]
-        high, lane = slot_cells(block)
-        lefts, rights = [], []
-        for k in range(q):
-            hit = rows_iota(halves_rows) == high[k : k + 1]
-            parts = halves(block[k : k + 1]) + halves(block[q + k : q + k + 1])
-            lefts.append(jnp.concatenate([jnp.where(hit, part, 0.0).astype(BF16) for part in parts], axis=0))
-            rights.append(one_hot(lane[k : k + 1], LANES))
-        total_ref[...] += dot_nt(jnp.concatenate(lefts, axis=1), jnp.concatenate(rights, axis=1))
+    group = 2
+
+    def add_blocks(step, carry):
+        for u in range(group):
+            origin = step * group + u
+            block = arrived[origin]
+            high, low = slot_cells(block)
+            lefts = []
+            for k in range(q):
+                hit = rows_iota(tile_rows) == high[k : k + 1]
+                parts = halves(block[k : k + 1]) + halves(block[q + k : q + k + 1])
+                lefts.append(jnp.concatenate([jnp.where(hit, p, 0.0) for p in parts], axis=0).astype(BF16))
+                column_hot[origin, :, k * LANES : (k + 1) * LANES] = one_hot(low[k : k + 1], tile_cols)
+            total_ref[...] += dot_nt(jnp.concatenate(lefts, axis=1), column_hot[origin])
         return carry
 
-    lax.fori_loop(0, places, add_block, 0)
-    h = halves_rows
+    lax.fori_loop(0, places // group, add_blocks, 0)
     for f in range(2):
-        both = total_ref[2 * f * h : (2 * f + 1) * h, :] + total_ref[(2 * f + 1) * h : (2 * f + 2) * h, :]
-        partial1[f, :, 0:LANES] = both[:tile_rows]
-        partial1[f, :, LANES : 2 * LANES] = both[tile_rows:]
+        start = 2 * f * tile_rows
+        partial1[f] = total_ref[start : start + tile_rows, :] + total_ref[start + tile_rows : start + 2 * tile_rows, :]
 
     my_rows = pl.multiple_of(mem * quarter, quarter)
 
@@ -397,34 +401,35 @@
     increment_ref[pl.ds(my_rows, quarter), :] = wide
     member_share(increment_ref, 0, 2)
 
-    field_value = increment_ref[...]
-    stacked = jnp.concatenate([field_value[:, :LANES], field_value[:, LANES:]], axis=0)
-    first, second = halves(stacked)
+    first, second = halves(increment_ref[...])
     lookup = jnp.concatenate([first, second], axis=0).astype(BF16)
 
-    def look(origin, carry):
-        high, lane_of = slot_cells(arrived[origin])
-        found = []
-        for k in range(q):
-            got = dot_nn(lookup, one_hot(lane_of[k : k + 1], LANES))
-            value = got[:halves_rows] + got[halves_rows:]
-            hit = rows_iota(halves_rows) == high[k : k + 1]
-            found.append(jnp.sum(jnp.where(hit, value, 0.0), axis=0, keepdims=True))
-        found.append(jnp.zeros((8 - q, LANES), F32))
-        answers[origin] = jnp.concatenate(found, axis=0)
+    def look(step, carry):
+        for u in range(group):
+            origin = step * group + u
+            high, low = slot_cells(arrived[origin])
+            got = dot_nn(lookup, column_hot[origin])
+            value = got[:tile_rows] + got[tile_rows:]
+            found = []
+            for k in range(q):
+                hit = rows_iota(tile_rows) == high[k : k + 1]
+                part = value[:, k * LANES : (k + 1) * LANES]
+                found.append(jnp.sum(jnp.where(hit, part, 0.0), axis=0, keepdims=True))
+            found.append(jnp.zeros((8 - q, LANES), F32))
+            answers[origin] = jnp.concatenate(found, axis=0)
         return carry
 
-    lax.fori_loop(0, places, look, 0)
+    lax.fori_loop(0, places // group, look, 0)
     exchange(answers, returned, a2a_sem.at[1])
     returned[place] = answers[place]
     exchange_wait(answers, returned, a2a_sem.at[1])
     first, second = halves(returned[...].reshape(places * 8, LANES))
     lookup = jnp.concatenate([first, second], axis=0).astype(BF16)
     answer_row = owner * 8 + lax.shift_right_logical(rank_ref[...], 7)
-    answer_lane = lax.bitwise_and(rank_ref[...], 127)
+    got = dot_nn(lookup, lane_hot[...])
+    values = got[: places * 8] + got[places * 8 :]
     for r in range(chunks):
-        got = dot_nn(lookup, one_hot(answer_lane[r : r + 1], LANES))
-        value = got[: places * 8] + got[places * 8 :]
+        value = values[:, r * LANES : (r + 1) * LANES]
         hit = rows_iota(places * 8) == answer_row[r : r + 1]
         found = jnp.sum(jnp.where(hit, value, 0.0), axis=0, keepdims=True)
         residual_ref[r : r + 1, :] = depart_ref[r : r + 1, :] - found
@@ -476,8 +481,10 @@
             vmem((places, 8, LANES), F32),
             vmem((places, 8, LANES), F32),
             vmem((rows, LANES), jnp.int32),
-            vmem((8 * tile_rows, LANES), F32),
+            vmem((4 * tile_rows, tile_cols), F32),
             vmem((2, ext, 384), F32),
+            vmem((LANES, count), BF16),
+            vmem((places, tile_cols, q * LANES), BF16),
         ] + [dma((8,))] * 8 + [dma((6, 2)), dma((2, 2))],
         compiler_params=pltpu.CompilerParams(
             collective_id=0, has_side_effects=True, vmem_limit_bytes=40 * 1024 * 1024

time: 62.3 us -> 60.5 us (0.971)
  Pallas kernels: 59 us -> 57.1 us
    pallas_call x1, Pallas kernels: 59 us -> 57.1 us  [per_device(): pl.pallas_call(functools.partial(kernel, (lat_size, lon_size, mem_size, p...]
where the time goes in v3:
time: 60.5 us; the launch traced here: 60.3 us
  Pallas kernels  57.1 us (94%)
  local copies, waits for them, and re-layouts  1.26 us (2%)
  other arithmetic  1.17 us (2%)
  between operations  0.74 us (1%)
    pallas_call x1, Pallas kernels, per_device(): pl.pallas_call(functools.partial(kernel, (lat_size, lon_size, mem_size, p...  57.1 us
    unnamed x14, local copies, waits for them, and re-layouts  1.26 us

profile of v3, /device:TPU:0, one launch (start us, length us, event | category | flops | bytes accessed | tf_op | source)
XLA Modules:
  0.0 60.3 jit_solution(11559249173566721581)
XLA Ops:
  0.6 0.0 copy-start
  0.6 0.0 copy-start.1
  0.7 0.0 copy-start.2
  0.7 0.0 copy-start.3
  0.7 0.0 copy-start.4
  0.7 0.0 copy-start.5
  0.7 1.2 %convert_bitcast_fusion.member_ref = f32[64,8,256]{2,1,0:T(8,128)S(1)} fusion(bf16[8,64,256]{2,1,0:T(8,128)(2,1)} %param.7), kind=kLoop, calls=%fused_computation | loop fusion | flops 131072 | bytes 786432 | tf_op jit(solution)/shard_map/convert_element_type | solution.py:455
  1.9 0.0 copy-done
  1.9 0.0 copy-done.1
  1.9 0.0 copy-done.2
  1.9 0.0 copy-done.3
  1.9 0.0 copy-done.4
  1.9 0.0 copy-done.5
  1.9 57.1 %update.1 = (f32[64,256]{1,0:T(8,128)S(1)}, f32[16,128]{1,0:T(8,128)S(1)}) custom-call(f32[64,8,256]{2,1,0:T(8,128)S(1)} %convert_bitcast_fusion.member_ref, f32[64,256]{1,0:T(8,128)S(1)} %copy-done, s32[64,256]{1,0:T(8,128)S(1)} %copy-done.1, s32[16,128]{1,0:T(8,128)S(1)} %bitcast.7, s32[16,128]{1,0:T(8,128)S(1)} %bitcast.8, f32[16,128]{1,0:T(8,128)S(1)} %bitcast.9, ...), custom_call_target="tpu_custom_call" | custom-call | tf_op jit(solution)/shard_map/update/pallas_call | solution.py:456
  59.1 0.6 %copy.13 = f32[64,256]{1,0:T(8,128)} copy(f32[64,256]{1,0:T(8,128)S(1)} %get-tuple-element.8) | data formatting | bytes 131072
  59.7 0.6 copy.14
Async XLA Ops:
  0.6 1.2 %copy-start = (f32[64,256]{1,0:T(8,128)S(1)}, f32[64,256]{1,0:T(8,128)}, u32[]{:S(2)}) copy-start(f32[64,256]{1,0:T(8,128)} %rate_ref.1) | copy-start | bytes 196612
  0.6 1.2 %copy-start.1 = (s32[64,256]{1,0:T(8,128)S(1)}, s32[64,256]{1,0:T(8,128)}, u32[]{:S(2)}) copy-start(s32[64,256]{1,0:T(8,128)} %sea_ref.1) | copy-start | bytes 196612
  0.7 1.2 %copy-start.2 = (s32[2048,1]{0,1:T(1,128)S(1)}, s32[2048,1]{0,1:T(1,128)}, u32[]{:S(2)}) copy-start(s32[2048,1]{0,1:T(1,128)} %param.10) | copy-start | bytes 24580
  0.7 1.2 %copy-start.3 = (s32[2048]{0:T(1024)S(1)}, s32[2048]{0:T(1024)}, u32[]{:S(2)}) copy-start(s32[2048]{0:T(1024)} %param.11) | copy-start | bytes 24580
  0.7 1.2 %copy-start.4 = (f32[2048]{0:T(1024)S(1)}, f32[2048]{0:T(1024)}, u32[]{:S(2)}) copy-start(f32[2048]{0:T(1024)} %param.12) | copy-start | bytes 24580
  0.7 1.2 %copy-start.5 = (f32[2048]{0:T(1024)S(1)}, f32[2048]{0:T(1024)}, u32[]{:S(2)}) copy-start(f32[2048]{0:T(1024)} %param.13) | copy-start | bytes 24580

commit v4 on v3

--- a/solution.py
+++ b/solution.py
@@ -14,6 +14,11 @@
 BF16 = jnp.bfloat16
 MESH = pl.DeviceIdType.MESH
 DIRECTIONS = [(0, 1), (0, -1), (1, 0), (-1, 0), (1, 1), (1, -1), (-1, 1), (-1, -1)]
+EVERY = range(8)
+SIDES = (0, 1, 4, 5, 6, 7)
+AHEAD = (2, 3)
+WIDE = {0: (pl.ds(0, 256), pl.ds(0, 256)), 1: (pl.ds(128, 128), pl.ds(384, 128)), -1: (pl.ds(0, 128), pl.ds(256, 128))}
+NARROW = {1: (pl.ds(0, 128), pl.ds(256, 128)), -1: (pl.ds(0, 128), pl.ds(128, 128))}
 
 
 def halves(value):
@@ -39,12 +44,12 @@
 
 def kernel(
     sizes,
-    member_ref, rate_ref, sea_ref, owner_ref, cell_ref, depart_ref, weight_ref,
+    member_ref, plain_ref, rate_ref, sea_ref, owner_ref, cell_ref, depart_ref, weight_ref,
     increment_ref, residual_ref,
-    member_ext, coef_ext, source1, source2, spread, member_all, north_all, east_all,
+    member_all, edge_ext, coef_ext, source1, source2, spread, north_all, east_all,
     outgoing, arrived, partial1, partial, gathered1, gathered2, gathered3, kept, answers, returned,
     rank_ref, total_ref, wide_ref, lane_hot, column_hot,
-    send_x, recv_x, send_c, recv_c, send_v1, recv_v1, send_v2, recv_v2, sums_sem, a2a_sem,
+    send_x, recv_x, send_e, recv_e, send_c, recv_c, send_v1, recv_v1, send_v2, recv_v2, sums_sem, a2a_sem,
 ):
     lat_size, lon_size, mem_size, places, q, block_rows, divisor = sizes
     tile_rows, tile_cols = rate_ref.shape
@@ -87,25 +92,38 @@
 
     @pl.when(lat == 0)
     def _():
-        member_ext[0:RIM] = jnp.zeros((RIM, 8, 512), F32)
+        member_all[0:RIM] = jnp.zeros((RIM, 8, 384), F32)
+        edge_ext[0:RIM] = jnp.zeros((RIM, 3 * LANES), F32)
 
     @pl.when(lat == lat_size - 1)
     def _():
-        member_ext[end:ext_rows] = jnp.zeros((RIM, 8, 512), F32)
-
-    member_ext[RIM:end, :, 0:tile_cols] = member_ref[...]
+        member_all[end:ext_rows] = jnp.zeros((RIM, 8, 384), F32)
+        edge_ext[end:ext_rows] = jnp.zeros((RIM, 3 * LANES), F32)
+
+    member_all[0:4, :, 0:tile_cols] = jnp.zeros((4, 8, tile_cols), F32)
+    member_all[end + 4 : ext_rows, :, 0:tile_cols] = jnp.zeros((4, 8, tile_cols), F32)
+    member_all[RIM:end, :, 0:tile_cols] = member_ref[...]
+    lane = lax.broadcasted_iota(jnp.int32, (1, LANES), 1)
+    edges = jnp.zeros((tile_rows, LANES), F32)
+    for m in range(8):
+        middle = 8 * (8 - m)
+        first_cols = plain_ref[m, :, 0:LANES].astype(F32)
+        last_cols = plain_ref[m, :, tile_cols - LANES : tile_cols].astype(F32)
+        turned = pltpu.roll(jnp.where(lane < 64, first_cols, last_cols), middle, 1)
+        edges = jnp.where((lane >= middle - 4) & (lane < middle + 4), turned, edges)
+    edge_ext[RIM:end, 0:LANES] = edges
     coef_ext[0, RIM:end, 0:tile_cols] = rate_ref[...]
     coef_ext[1, RIM:end, 0:tile_cols] = sea_ref[...].astype(F32)
 
     pl.semaphore_wait(barrier, places - 1 + mem_size - 1)
 
-    def halo_copies(at, send_sem, recv_sem):
+    def halo_copies(at, send_sem, recv_sem, directions, depth=RIM, cols=None):
         made = []
-        for k, (dy, dx) in enumerate(DIRECTIONS):
-            source_rows = {0: pl.ds(RIM, tile_rows), 1: pl.ds(end - RIM, RIM), -1: pl.ds(RIM, RIM)}[dy]
-            target_rows = {0: pl.ds(RIM, tile_rows), 1: pl.ds(0, RIM), -1: pl.ds(end, RIM)}[dy]
-            source_cols = {0: pl.ds(0, 256), 1: pl.ds(128, 128), -1: pl.ds(0, 128)}[dx]
-            target_cols = {0: pl.ds(0, 256), 1: pl.ds(384, 128), -1: pl.ds(256, 128)}[dx]
+        for k in directions:
+            dy, dx = DIRECTIONS[k]
+            source_rows = {0: pl.ds(RIM, tile_rows), 1: pl.ds(end - depth, depth), -1: pl.ds(RIM, depth)}[dy]
+            target_rows = {0: pl.ds(RIM, tile_rows), 1: pl.ds(RIM - depth, depth), -1: pl.ds(end, depth)}[dy]
+            source_cols, target_cols = (cols or WIDE)[dx]
             copy = pltpu.make_async_remote_copy(
                 src_ref=at(source_rows, source_cols),
                 dst_ref=at(target_rows, target_cols),
@@ -129,16 +147,19 @@
         for copy, sends, gets in copies:
             when(sends, lambda copy=copy: copy.start())
 
+    sent = []
+
     def halo_wait(copies):
         for copy, sends, gets in copies:
-            when(sends, lambda copy=copy: copy.wait_send())
             when(gets, lambda copy=copy: copy.wait_recv())
-
-    coef_copies = halo_copies(lambda r, c: coef_ext.at[:, r, c], send_c, recv_c)
-    member_copies = halo_copies(lambda r, c: member_ext.at[r, :, c], send_x, recv_x)
+            sent.append(lambda copy=copy, sends=sends: when(sends, lambda: copy.wait_send()))
+
+    coef_copies = halo_copies(lambda r, c: coef_ext.at[:, r, c], send_c, recv_c, EVERY)
+    edge_copies = halo_copies(lambda r, c: edge_ext.at[r, c], send_e, recv_e, SIDES, cols=NARROW)
+    member_copies = halo_copies(lambda r, c: member_all.at[r, :, c], send_x, recv_x, AHEAD, depth=4)
     source_copies = [
-        halo_copies(lambda r, c: source1.at[r, c], send_v1, recv_v1),
-        halo_copies(lambda r, c: source2.at[r, c], send_v2, recv_v2),
+        halo_copies(lambda r, c: source1.at[r, c], send_v1, recv_v1, EVERY),
+        halo_copies(lambda r, c: source2.at[r, c], send_v2, recv_v2, EVERY),
     ]
 
     owner = owner_ref[...]
@@ -209,11 +230,12 @@
             send_sem=sems.at[0], recv_sem=sems.at[1],
             device_id=place_at(1)[1], device_id_type=MESH,
         )
-        whole.wait_send()
         whole.wait_recv()
+        sent.append(whole.wait_send)
 
     exchange(outgoing, arrived, a2a_sem.at[0])
     halo_start(coef_copies)
+    halo_start(edge_copies)
     halo_start(member_copies)
     arrived[place] = outgoing[place]
     exchange_wait(outgoing, arrived, a2a_sem.at[0])
@@ -268,8 +290,8 @@
             send_sem=sems.at[0], recv_sem=sems.at[1],
             device_id=(lat, lon, lax.rem(mem + 1, mem_size)), device_id_type=MESH,
         )
-        whole.wait_send()
         whole.wait_recv()
+        sent.append(whole.wait_send)
         total = got[0]
         for other in range(1, mem_size):
             total = total + got[other]
@@ -289,8 +311,8 @@
             src_ref=rest, dst_ref=rest, send_sem=sems.at[0], recv_sem=sems.at[1],
             device_id=(lat, lon, lax.rem(mem + 1, mem_size)), device_id_type=MESH,
         )
-        whole.wait_send()
         whole.wait_recv()
+        sent.append(whole.wait_send)
 
     first_part = lambda rows: partial1.at[:, rows]
     for step in range(1, mem_size):
@@ -301,13 +323,13 @@
     member_share(source1, RIM, 0)
     halo_start(source_copies[0])
 
-    lane = lax.broadcasted_iota(jnp.int32, (1, LANES), 1)
 
     def joined(value):
         side = jnp.where(lane < 64, value[..., 256:384], value[..., 384:512])
         return jnp.concatenate([value[..., 0:256], side], axis=-1)
 
     halo_wait(coef_copies)
+    halo_wait(edge_copies)
     halo_wait(member_copies)
     rate = joined(coef_ext[0])
     sea = joined(coef_ext[1])
@@ -322,10 +344,11 @@
             i = base + u
             north_all[i] = jnp.broadcast_to(wide_ref[0, pl.ds(i, 1), :], (8, width))
             east_all[i] = jnp.broadcast_to(wide_ref[1, pl.ds(i, 1), :], (8, width))
-            value = member_ext[i]
-            side = jnp.where(lane < 64, value[:, 256:384], value[:, 384:512])
-            member_all[i, :, 0:256] = value[:, 0:256]
-            member_all[i, :, 256:384] = side
+            line = edge_ext[pl.ds(i, 1), :]
+            both = jnp.where(lax.bitwise_and(lane, 7) < 4, line[:, 128:256], line[:, 256:384])
+            member_all[i, :, 256:384] = pltpu.roll(
+                jnp.broadcast_to(both, (8, LANES)), 64, 1, stride=8, stride_axis=0
+            )
         return carry
 
     lax.fori_loop(0, ext_rows // 8, widen, 0)
@@ -391,11 +414,14 @@
     halo_wait(source_copies[0])
     later_part = lambda rows: partial.at[rows]
     covariance(source1, lambda part: sum_part(later_part, gathered2, 1, part))
-    first_pass = my_sea() * member_sum(later_part, gathered2, 1) / divisor
+    first_total = member_sum(later_part, gathered2, 1)
+    sum_sent = sent.pop()
+    first_pass = my_sea() * first_total / divisor
     source2[pl.ds(RIM + my_rows, quarter), 0:tile_cols] = kept[0] - kept[1] * first_pass
     member_share(source2, RIM, 1)
     halo_start(source_copies[1])
     halo_wait(source_copies[1])
+    sum_sent()
     covariance(source2, lambda part: sum_part(later_part, gathered3, 2, part))
     wide = my_sea() * member_sum(later_part, gathered3, 2) / divisor
     increment_ref[pl.ds(my_rows, quarter), :] = wide
@@ -433,6 +459,8 @@
         hit = rows_iota(places * 8) == answer_row[r : r + 1]
         found = jnp.sum(jnp.where(hit, value, 0.0), axis=0, keepdims=True)
         residual_ref[r : r + 1, :] = depart_ref[r : r + 1, :] - found
+    for wait in sent:
+        wait()
 
 
 def per_device(sizes, perturbations, diffusivity, sea_mask, obs_owner, obs_cell, obs_depart, obs_weight):
@@ -459,14 +487,14 @@
             jax.ShapeDtypeStruct((tile_rows, tile_cols), F32),
             jax.ShapeDtypeStruct((rows, LANES), F32),
         ),
-        in_specs=[pl.BlockSpec(memory_space=vmem)] * 7,
+        in_specs=[pl.BlockSpec(memory_space=vmem)] * 8,
         out_specs=(pl.BlockSpec(memory_space=vmem),) * 2,
         scratch_shapes=[
-            vmem((ext, 8, 512), F32),
+            vmem((ext, 8, 384), F32),
+            vmem((ext, 3 * LANES), F32),
             vmem((2, ext, 512), F32),
             vmem((ext, 512), F32),
             vmem((ext, 512), F32),
-            vmem((ext, 8, 384), F32),
             vmem((ext, 8, 384), F32),
             vmem((ext, 8, 384), F32),
             vmem((ext, 8, 384), F32),
@@ -485,13 +513,13 @@
             vmem((2, ext, 384), F32),
             vmem((LANES, count), BF16),
             vmem((places, tile_cols, q * LANES), BF16),
-        ] + [dma((8,))] * 8 + [dma((6, 2)), dma((2, 2))],
+        ] + [dma((8,))] * 10 + [dma((6, 2)), dma((2, 2))],
         compiler_params=pltpu.CompilerParams(
             collective_id=0, has_side_effects=True, vmem_limit_bytes=40 * 1024 * 1024
         ),
         name="update",
     )(
-        member_rows, diffusivity, sea_mask,
+        member_rows, perturbations, diffusivity, sea_mask,
         as_rows(obs_owner), as_rows(obs_cell), as_rows(obs_depart), as_rows(obs_weight),
     )
     return increment, residual.reshape(count)

time: 60.5 us -> 60.3 us (level)
    unnamed x14 -> x16, local copies, waits for them, and re-layouts: 1.26 us -> 1.26 us
where the time goes in v4:
time: 60.3 us; the launch traced here: 60.2 us
  Pallas kernels  57 us (95%)
  local copies, waits for them, and re-layouts  1.26 us (2%)
  other arithmetic  1.16 us (2%)
  between operations  0.75 us (1%)
    pallas_call x1, Pallas kernels, per_device(): pl.pallas_call(functools.partial(kernel, (lat_size, lon_size, mem_size, p...  57 us
    unnamed x16, local copies, waits for them, and re-layouts  1.26 us

profile of v4, /device:TPU:0, one launch (start us, length us, event | category | flops | bytes accessed | tf_op | source)
XLA Modules:
  0.0 60.2 jit_solution(11502163808896232122)
XLA Ops:
  0.6 0.0 copy-start
  0.6 0.0 copy-start.1
  0.7 0.0 copy-start.2
  0.7 0.0 copy-start.3
  0.7 0.0 copy-start.4
  0.7 0.0 copy-start.5
  0.7 0.0 copy-start.6
  0.7 1.2 %convert_bitcast_fusion.member_ref = f32[64,8,256]{2,1,0:T(8,128)S(1)} fusion(bf16[8,64,256]{2,1,0:T(8,128)(2,1)} %plain_ref.1), kind=kLoop, calls=%fused_computation | loop fusion | flops 131072 | bytes 786432 | tf_op jit(solution)/shard_map/convert_element_type | solution.py:483
  1.9 0.0 copy-done
  1.9 0.0 copy-done.1
  1.9 0.0 copy-done.2
  1.9 0.0 copy-done.3
  1.9 0.0 copy-done.4
  1.9 0.0 copy-done.5
  1.9 0.0 copy-done.6
  1.9 57.0 %update.1 = (f32[64,256]{1,0:T(8,128)S(1)}, f32[16,128]{1,0:T(8,128)S(1)}) custom-call(f32[64,8,256]{2,1,0:T(8,128)S(1)} %convert_bitcast_fusion.member_ref, bf16[8,64,256]{2,1,0:T(8,128)(2,1)S(1)} %copy-done, f32[64,256]{1,0:T(8,128)S(1)} %copy-done.1, s32[64,256]{1,0:T(8,128)S(1)} %copy-done.2, s32[16,128]{1,0:T(8,128)S(1)} %bitcast.8, ...), custom_call_target="tpu_custom_call" | custom-call | tf_op jit(solution)/shard_map/update/pallas_call | solution.py:484
  58.9 0.6 %copy.13 = f32[64,256]{1,0:T(8,128)} copy(f32[64,256]{1,0:T(8,128)S(1)} %get-tuple-element.8) | data formatting | bytes 131072
  59.6 0.6 copy.14
Async XLA Ops:
  0.6 1.2 %copy-start = (bf16[8,64,256]{2,1,0:T(8,128)(2,1)S(1)}, bf16[8,64,256]{2,1,0:T(8,128)(2,1)}, u32[]{:S(2)}) copy-start(bf16[8,64,256]{2,1,0:T(8,128)(2,1)} %plain_ref.1) | copy-start | bytes 786436
  0.6 1.2 %copy-start.1 = (f32[64,256]{1,0:T(8,128)S(1)}, f32[64,256]{1,0:T(8,128)}, u32[]{:S(2)}) copy-start(f32[64,256]{1,0:T(8,128)} %rate_ref.1) | copy-start | bytes 196612
  0.7 1.2 %copy-start.2 = (s32[64,256]{1,0:T(8,128)S(1)}, s32[64,256]{1,0:T(8,128)}, u32[]{:S(2)}) copy-start(s32[64,256]{1,0:T(8,128)} %sea_ref.1) | copy-start | bytes 196612
  0.7 1.2 %copy-start.3 = (s32[2048,1]{0,1:T(1,128)S(1)}, s32[2048,1]{0,1:T(1,128)}, u32[]{:S(2)}) copy-start(s32[2048,1]{0,1:T(1,128)} %param.10) | copy-start | bytes 24580
  0.7 1.2 %copy-start.4 = (s32[2048]{0:T(1024)S(1)}, s32[2048]{0:T(1024)}, u32[]{:S(2)}) copy-start(s32[2048]{0:T(1024)} %param.11) | copy-start | bytes 24580
  0.7 1.2 %copy-start.5 = (f32[2048]{0:T(1024)S(1)}, f32[2048]{0:T(1024)}, u32[]{:S(2)}) copy-start(f32[2048]{0:T(1024)} %param.12) | copy-start | bytes 24580
  0.7 1.2 %copy-start.6 = (f32[2048]{0:T(1024)S(1)}, f32[2048]{0:T(1024)}, u32[]{:S(2)}) copy-start(f32[2048]{0:T(1024)} %param.13) | copy-start | bytes 24580

commit v5 on v4

--- a/solution.py
+++ b/solution.py
@@ -46,7 +46,7 @@
     sizes,
     member_ref, plain_ref, rate_ref, sea_ref, owner_ref, cell_ref, depart_ref, weight_ref,
     increment_ref, residual_ref,
-    member_all, edge_ext, coef_ext, source1, source2, spread, north_all, east_all,
+    member_all, edge_ext, coef_ext, source1, source2, spread, north_all, east_all, west_all,
     outgoing, arrived, partial1, partial, gathered1, gathered2, gathered3, kept, answers, returned,
     rank_ref, total_ref, wide_ref, lane_hot, column_hot,
     send_x, recv_x, send_e, recv_e, send_c, recv_c, send_v1, recv_v1, send_v2, recv_v2, sums_sem, a2a_sem,
@@ -245,20 +245,22 @@
         return lax.shift_right_logical(whole, 8), lax.bitwise_and(whole, 255)
 
     total_ref[...] = jnp.zeros_like(total_ref)
-    group = 2
+    group = 4
+    span = q * LANES
 
     def add_blocks(step, carry):
+        lefts, rights = [], []
         for u in range(group):
-            origin = step * group + u
-            block = arrived[origin]
+            block = arrived[step * group + u]
             high, low = slot_cells(block)
-            lefts = []
             for k in range(q):
                 hit = rows_iota(tile_rows) == high[k : k + 1]
                 parts = halves(block[k : k + 1]) + halves(block[q + k : q + k + 1])
                 lefts.append(jnp.concatenate([jnp.where(hit, p, 0.0) for p in parts], axis=0).astype(BF16))
-                column_hot[origin, :, k * LANES : (k + 1) * LANES] = one_hot(low[k : k + 1], tile_cols)
-            total_ref[...] += dot_nt(jnp.concatenate(lefts, axis=1), column_hot[origin])
+                rights.append(one_hot(low[k : k + 1], tile_cols))
+        right = jnp.concatenate(rights, axis=1)
+        column_hot[step] = right
+        total_ref[...] += dot_nt(jnp.concatenate(lefts, axis=1), right)
         return carry
 
     lax.fori_loop(0, places // group, add_blocks, 0)
@@ -338,12 +340,15 @@
     wide_ref[0] = 0.5 * (rate + below(rate)) * sea * below(sea)
     wide_ref[1] = 0.5 * (rate + pltpu.roll(rate, width - 1, 1)) * sea * pltpu.roll(sea, width - 1, 1)
 
+    wide_ref[2] = pltpu.roll(wide_ref[1], 1, 1)
+
     def widen(step, carry):
         base = pl.multiple_of(step * 8, 8)
         for u in range(8):
             i = base + u
             north_all[i] = jnp.broadcast_to(wide_ref[0, pl.ds(i, 1), :], (8, width))
             east_all[i] = jnp.broadcast_to(wide_ref[1, pl.ds(i, 1), :], (8, width))
+            west_all[i] = jnp.broadcast_to(wide_ref[2, pl.ds(i, 1), :], (8, width))
             line = edge_ext[pl.ds(i, 1), :]
             both = jnp.where(lax.bitwise_and(lane, 7) < 4, line[:, 128:256], line[:, 256:384])
             member_all[i, :, 256:384] = pltpu.roll(
@@ -364,7 +369,8 @@
                 here, after = values[u], values[u + 1]
                 flux_after = north_all[base + u] * (after - here)
                 flux_east = east_all[base + u] * (pltpu.roll(here, width - 1, 1) - here)
-                results.append(here + (flux_after - flux) + (flux_east - pltpu.roll(flux_east, 1, 1)))
+                flux_west = west_all[base + u] * (pltpu.roll(here, 1, 1) - here)
+                results.append(here + (flux_after - flux) + (flux_east + flux_west))
                 flux = flux_after
             return results, (values[-1], flux)
 
@@ -374,13 +380,13 @@
 
         def sweep(read):
             def rows(step, carry):
-                base = 4 + step * 8
-                results, carry = step_rows(read, base, carry, 8)
-                for u in range(8):
+                base = 4 + step * 24
+                results, carry = step_rows(read, base, carry, 24)
+                for u in range(24):
                     spread[base + u] = results[u]
                 return carry
 
-            lax.fori_loop(0, (tile_rows + 8) // 8, rows, first_of(read, 4))
+            lax.fori_loop(0, (tile_rows + 8) // 24, rows, first_of(read, 4))
 
         def begin(i):
             return member_all[i] * wide_ref[0, pl.ds(i, 1), :]
@@ -394,20 +400,15 @@
         for turn in range(STEPS - 2):
             sweep(again)
 
-        def last_rows(step, carry):
-            base = RIM + step * 8
-            results, carry = step_rows(again, base, carry, 8)
+        carry = first_of(again, RIM)
+        for part in range(mem_size):
+            base = RIM + part * quarter
+            results, carry = step_rows(again, base, carry, quarter)
             found = [
                 jnp.sum(results[u][:, 0:256] * member_all[base + u, :, 0:256], axis=0, keepdims=True)
-                for u in range(8)
+                for u in range(quarter)
             ]
-            partial[pl.ds(pl.multiple_of(step * 8, 8), 8), :] = jnp.concatenate(found, axis=0)
-            return carry
-
-        carry = first_of(again, RIM)
-        steps = quarter // 8
-        for part in range(mem_size):
-            carry = lax.fori_loop(part * steps, (part + 1) * steps, last_rows, carry)
+            partial[part * quarter : (part + 1) * quarter, :] = jnp.concatenate(found, axis=0)
             finished(part)
 
     my_sea = lambda: coef_ext[1, pl.ds(RIM + my_rows, quarter), 0:tile_cols]
@@ -431,15 +432,16 @@
     lookup = jnp.concatenate([first, second], axis=0).astype(BF16)
 
     def look(step, carry):
+        got = dot_nn(lookup, column_hot[step])
+        value = got[:tile_rows] + got[tile_rows:]
         for u in range(group):
             origin = step * group + u
             high, low = slot_cells(arrived[origin])
-            got = dot_nn(lookup, column_hot[origin])
-            value = got[:tile_rows] + got[tile_rows:]
             found = []
             for k in range(q):
                 hit = rows_iota(tile_rows) == high[k : k + 1]
-                part = value[:, k * LANES : (k + 1) * LANES]
+                start = u * span + k * LANES
+                part = value[:, start : start + LANES]
                 found.append(jnp.sum(jnp.where(hit, part, 0.0), axis=0, keepdims=True))
             found.append(jnp.zeros((8 - q, LANES), F32))
             answers[origin] = jnp.concatenate(found, axis=0)
@@ -498,6 +500,7 @@
             vmem((ext, 8, 384), F32),
             vmem((ext, 8, 384), F32),
             vmem((ext, 8, 384), F32),
+            vmem((ext, 8, 384), F32),
             vmem((places, block_rows, LANES), F32),
             vmem((places, block_rows, LANES), F32),
             vmem((2, tile_rows, tile_cols), F32),
@@ -510,9 +513,9 @@
             vmem((places, 8, LANES), F32),
             vmem((rows, LANES), jnp.int32),
             vmem((4 * tile_rows, tile_cols), F32),
-            vmem((2, ext, 384), F32),
+            vmem((3, ext, 384), F32),
             vmem((LANES, count), BF16),
-            vmem((places, tile_cols, q * LANES), BF16),
+            vmem((places // 4, tile_cols, 4 * q * LANES), BF16),
         ] + [dma((8,))] * 10 + [dma((6, 2)), dma((2, 2))],
         compiler_params=pltpu.CompilerParams(
             collective_id=0, has_side_effects=True, vmem_limit_bytes=40 * 1024 * 1024

time: 60.3 us -> 54 us (0.90)
  Pallas kernels: 57 us -> 50.7 us
    pallas_call x1, Pallas kernels: 57 us -> 50.7 us  [per_device(): pl.pallas_call(functools.partial(kernel, (lat_size, lon_size, mem_size, p...]
where the time goes in v5:
time: 54 us; the launch traced here: 53.8 us
  Pallas kernels  50.7 us (94%)
  local copies, waits for them, and re-layouts  1.26 us (2%)
  other arithmetic  1.16 us (2%)
  between operations  0.75 us (1%)
    pallas_call x1, Pallas kernels, per_device(): pl.pallas_call(functools.partial(kernel, (lat_size, lon_size, mem_size, p...  50.7 us
    unnamed x16, local copies, waits for them, and re-layouts  1.26 us
    convert_element_type x1, other arithmetic, per_device(): member_rows = jnp.transpose(perturbations, (1, 0, 2)).astype(F32)  1.16 us

profile of v5, /device:TPU:0, one launch (start us, length us, event | category | flops | bytes accessed | tf_op | source)
XLA Modules:
  0.0 53.8 jit_solution(9858390195999836412)
XLA Ops:
  0.6 0.0 copy-start
  0.6 0.0 copy-start.1
  0.7 0.0 copy-start.2
  0.7 0.0 copy-start.3
  0.7 0.0 copy-start.4
  0.7 0.0 copy-start.5
  0.7 0.0 copy-start.6
  0.7 1.2 %convert_bitcast_fusion.member_ref = f32[64,8,256]{2,1,0:T(8,128)S(1)} fusion(bf16[8,64,256]{2,1,0:T(8,128)(2,1)} %plain_ref.1), kind=kLoop, calls=%fused_computation | loop fusion | flops 131072 | bytes 786432 | tf_op jit(solution)/shard_map/convert_element_type | solution.py:485
  1.9 0.0 copy-done
  1.9 0.0 copy-done.1
  1.9 0.0 copy-done.2
  1.9 0.0 copy-done.3
  1.9 0.0 copy-done.4
  1.9 0.0 copy-done.5
  1.9 0.0 copy-done.6
  1.9 50.7 %update.1 = (f32[64,256]{1,0:T(8,128)S(1)}, f32[16,128]{1,0:T(8,128)S(1)}) custom-call(f32[64,8,256]{2,1,0:T(8,128)S(1)} %convert_bitcast_fusion.member_ref, bf16[8,64,256]{2,1,0:T(8,128)(2,1)S(1)} %copy-done, f32[64,256]{1,0:T(8,128)S(1)} %copy-done.1, s32[64,256]{1,0:T(8,128)S(1)} %copy-done.2, s32[16,128]{1,0:T(8,128)S(1)} %bitcast.8, ...), custom_call_target="tpu_custom_call" | custom-call | tf_op jit(solution)/shard_map/update/pallas_call | solution.py:486
  52.6 0.6 %copy.13 = f32[64,256]{1,0:T(8,128)} copy(f32[64,256]{1,0:T(8,128)S(1)} %get-tuple-element.8) | data formatting | bytes 131072
  53.2 0.6 %copy.14 = f32[2048]{0:T(1024)} copy(f32[2048]{0:T(1024)S(1)} %bitcast.7) | data formatting | bytes 16384
Async XLA Ops:
  0.6 1.2 %copy-start = (bf16[8,64,256]{2,1,0:T(8,128)(2,1)S(1)}, bf16[8,64,256]{2,1,0:T(8,128)(2,1)}, u32[]{:S(2)}) copy-start(bf16[8,64,256]{2,1,0:T(8,128)(2,1)} %plain_ref.1) | copy-start | bytes 786436
  0.6 1.2 %copy-start.1 = (f32[64,256]{1,0:T(8,128)S(1)}, f32[64,256]{1,0:T(8,128)}, u32[]{:S(2)}) copy-start(f32[64,256]{1,0:T(8,128)} %rate_ref.1) | copy-start | bytes 196612
  0.7 1.2 %copy-start.2 = (s32[64,256]{1,0:T(8,128)S(1)}, s32[64,256]{1,0:T(8,128)}, u32[]{:S(2)}) copy-start(s32[64,256]{1,0:T(8,128)} %sea_ref.1) | copy-start | bytes 196612
  0.7 1.2 %copy-start.3 = (s32[2048,1]{0,1:T(1,128)S(1)}, s32[2048,1]{0,1:T(1,128)}, u32[]{:S(2)}) copy-start(s32[2048,1]{0,1:T(1,128)} %param.10) | copy-start | bytes 24580
  0.7 1.2 %copy-start.4 = (s32[2048]{0:T(1024)S(1)}, s32[2048]{0:T(1024)}, u32[]{:S(2)}) copy-start(s32[2048]{0:T(1024)} %param.11) | copy-start | bytes 24580
  0.7 1.2 %copy-start.5 = (f32[2048]{0:T(1024)S(1)}, f32[2048]{0:T(1024)}, u32[]{:S(2)}) copy-start(f32[2048]{0:T(1024)} %param.12) | copy-start | bytes 24580
  0.7 1.2 %copy-start.6 = (f32[2048]{0:T(1024)S(1)}, f32[2048]{0:T(1024)}, u32[]{:S(2)}) copy-start(f32[2048]{0:T(1024)} %param.13) | copy-start | bytes 24580

commit v6 on v5

--- a/solution.py
+++ b/solution.py
@@ -68,6 +68,15 @@
         other = lax.rem(place + step, places)
         return other, (other // lon_size, lax.rem(other, lon_size), mem)
 
+    def when(condition, action):
+        if condition is None:
+            action()
+        else:
+            pl.when(condition)(action)
+
+    def neighbour(dy, dx, member):
+        return lat + dy, lax.rem(lon + dx + lon_size, lon_size), member
+
     barrier = pltpu.get_barrier_semaphore()
 
     def greet(step, carry):
@@ -79,6 +88,13 @@
         pl.semaphore_signal(
             barrier, inc=1, device_id=(lat, lon, lax.rem(mem + step, mem_size)), device_id_type=MESH
         )
+
+    exists = {0: None, 1: lat < lat_size - 1, -1: lat > 0}
+    for dy, dx in DIRECTIONS:
+        for step in range(1, mem_size):
+            when(exists[dy], lambda dy=dy, dx=dx, step=step: pl.semaphore_signal(
+                barrier, inc=1, device_id=neighbour(dy, dx, lax.rem(mem + step, mem_size)), device_id_type=MESH
+            ))
 
     zero_rows = jnp.zeros((RIM, 512), F32)
     for ext in (source1, source2, coef_ext.at[0], coef_ext.at[1]):
@@ -115,8 +131,6 @@
     coef_ext[0, RIM:end, 0:tile_cols] = rate_ref[...]
     coef_ext[1, RIM:end, 0:tile_cols] = sea_ref[...].astype(F32)
 
-    pl.semaphore_wait(barrier, places - 1 + mem_size - 1)
-
     def halo_copies(at, send_sem, recv_sem, directions, depth=RIM, cols=None):
         made = []
         for k in directions:
@@ -129,19 +143,13 @@
                 dst_ref=at(target_rows, target_cols),
                 send_sem=send_sem.at[k],
                 recv_sem=recv_sem.at[k],
-                device_id=(lat + dy, lax.rem(lon + dx + lon_size, lon_size), mem),
+                device_id=neighbour(dy, dx, mem),
                 device_id_type=MESH,
             )
             sends = {0: None, 1: lat < lat_size - 1, -1: lat > 0}[dy]
             gets = {0: None, 1: lat > 0, -1: lat < lat_size - 1}[dy]
             made.append((copy, sends, gets))
         return made
-
-    def when(condition, action):
-        if condition is None:
-            action()
-        else:
-            pl.when(condition)(action)
 
     def halo_start(copies):
         for copy, sends, gets in copies:
@@ -233,6 +241,8 @@
         whole.wait_recv()
         sent.append(whole.wait_send)
 
+    tiles = 2 + 3 * (jnp.where(lat > 0, 1, 0) + jnp.where(lat < lat_size - 1, 1, 0))
+    pl.semaphore_wait(barrier, places - 1 + (mem_size - 1) * (tiles + 1))
     exchange(outgoing, arrived, a2a_sem.at[0])
     halo_start(coef_copies)
     halo_start(edge_copies)
@@ -299,7 +309,27 @@
             total = total + got[other]
         return total
 
-    def member_share(ref, first, number):
+    def edge_share(ref, send_sem, recv_sem):
+        own = pl.ds(RIM + my_rows, quarter)
+        for k, (dy, dx) in enumerate(DIRECTIONS):
+            source_rows = {0: own, 1: pl.ds(end - RIM, RIM), -1: pl.ds(RIM, RIM)}[dy]
+            target_rows = {0: own, 1: pl.ds(0, RIM), -1: pl.ds(end, RIM)}[dy]
+            source_cols, target_cols = WIDE[dx]
+            sends = {0: None, 1: (lat < lat_size - 1) & (mem == mem_size - 1), -1: (lat > 0) & (mem == 0)}[dy]
+            for step in range(mem_size):
+                copy = pltpu.make_async_remote_copy(
+                    src_ref=ref.at[source_rows, source_cols], dst_ref=ref.at[target_rows, target_cols],
+                    send_sem=send_sem.at[k * mem_size + step], recv_sem=recv_sem.at[k],
+                    device_id=neighbour(dy, dx, lax.rem(mem + step, mem_size)), device_id_type=MESH,
+                )
+                when(sends, lambda copy=copy: copy.start())
+                sent.append(lambda copy=copy, sends=sends: when(sends, lambda: copy.wait_send()))
+
+    def edge_wait(copies):
+        for copy, sends, gets in copies:
+            when(gets, lambda copy=copy: copy.wait_recv())
+
+    def member_share(ref, first, number, meanwhile=lambda: None):
         sems = sums_sem.at[2 * number + 1]
         mine = ref.at[pl.ds(first + my_rows, quarter), pl.ds(0, tile_cols)]
         for step in range(1, mem_size):
@@ -308,6 +338,7 @@
                 send_sem=sems.at[0], recv_sem=sems.at[1],
                 device_id=(lat, lon, lax.rem(mem + step, mem_size)), device_id_type=MESH,
             ).start()
+        meanwhile()
         rest = ref.at[pl.ds(first, (mem_size - 1) * quarter), pl.ds(0, tile_cols)]
         whole = pltpu.make_async_remote_copy(
             src_ref=rest, dst_ref=rest, send_sem=sems.at[0], recv_sem=sems.at[1],
@@ -322,41 +353,44 @@
     summed = member_sum(first_part, gathered1, 0)
     kept[...] = summed
     source1[pl.ds(RIM + my_rows, quarter), 0:tile_cols] = summed[0]
-    member_share(source1, RIM, 0)
-    halo_start(source_copies[0])
-
+
+    width = 384
 
     def joined(value):
         side = jnp.where(lane < 64, value[..., 256:384], value[..., 384:512])
         return jnp.concatenate([value[..., 0:256], side], axis=-1)
 
-    halo_wait(coef_copies)
-    halo_wait(edge_copies)
-    halo_wait(member_copies)
-    rate = joined(coef_ext[0])
-    sea = joined(coef_ext[1])
-    below = lambda a: jnp.concatenate([a[1:], a[:1]], axis=0)
-    width = 384
-    wide_ref[0] = 0.5 * (rate + below(rate)) * sea * below(sea)
-    wide_ref[1] = 0.5 * (rate + pltpu.roll(rate, width - 1, 1)) * sea * pltpu.roll(sea, width - 1, 1)
-
-    wide_ref[2] = pltpu.roll(wide_ref[1], 1, 1)
-
-    def widen(step, carry):
-        base = pl.multiple_of(step * 8, 8)
-        for u in range(8):
-            i = base + u
-            north_all[i] = jnp.broadcast_to(wide_ref[0, pl.ds(i, 1), :], (8, width))
-            east_all[i] = jnp.broadcast_to(wide_ref[1, pl.ds(i, 1), :], (8, width))
-            west_all[i] = jnp.broadcast_to(wide_ref[2, pl.ds(i, 1), :], (8, width))
-            line = edge_ext[pl.ds(i, 1), :]
-            both = jnp.where(lax.bitwise_and(lane, 7) < 4, line[:, 128:256], line[:, 256:384])
-            member_all[i, :, 256:384] = pltpu.roll(
-                jnp.broadcast_to(both, (8, LANES)), 64, 1, stride=8, stride_axis=0
-            )
-        return carry
-
-    lax.fori_loop(0, ext_rows // 8, widen, 0)
+    def prepare():
+        edge_share(source1, send_v1, recv_v1)
+        halo_wait(coef_copies)
+        halo_wait(edge_copies)
+        halo_wait(member_copies)
+        rate = joined(coef_ext[0])
+        sea = joined(coef_ext[1])
+        below = lambda a: jnp.concatenate([a[1:], a[:1]], axis=0)
+        wide_ref[0] = 0.5 * (rate + below(rate)) * sea * below(sea)
+        wide_ref[1] = 0.5 * (rate + pltpu.roll(rate, width - 1, 1)) * sea * pltpu.roll(sea, width - 1, 1)
+
+        wide_ref[2] = pltpu.roll(wide_ref[1], 1, 1)
+
+        def widen(step, carry):
+            base = pl.multiple_of(step * 8, 8)
+            for u in range(8):
+                i = base + u
+                north_all[i] = jnp.broadcast_to(wide_ref[0, pl.ds(i, 1), :], (8, width))
+                east_all[i] = jnp.broadcast_to(wide_ref[1, pl.ds(i, 1), :], (8, width))
+                west_all[i] = jnp.broadcast_to(wide_ref[2, pl.ds(i, 1), :], (8, width))
+                line = edge_ext[pl.ds(i, 1), :]
+                both = jnp.where(lax.bitwise_and(lane, 7) < 4, line[:, 128:256], line[:, 256:384])
+                member_all[i, :, 256:384] = pltpu.roll(
+                    jnp.broadcast_to(both, (8, LANES)), 64, 1, stride=8, stride_axis=0
+                )
+            return carry
+
+        lax.fori_loop(0, ext_rows // 8, widen, 0)
+
+    member_share(source1, RIM, 0, prepare)
+    edge_wait(source_copies[0])
 
     def covariance(source, finished):
         wide_ref[0] = joined(source[...])
@@ -412,16 +446,14 @@
             finished(part)
 
     my_sea = lambda: coef_ext[1, pl.ds(RIM + my_rows, quarter), 0:tile_cols]
-    halo_wait(source_copies[0])
     later_part = lambda rows: partial.at[rows]
     covariance(source1, lambda part: sum_part(later_part, gathered2, 1, part))
     first_total = member_sum(later_part, gathered2, 1)
     sum_sent = sent.pop()
     first_pass = my_sea() * first_total / divisor
     source2[pl.ds(RIM + my_rows, quarter), 0:tile_cols] = kept[0] - kept[1] * first_pass
-    member_share(source2, RIM, 1)
-    halo_start(source_copies[1])
-    halo_wait(source_copies[1])
+    member_share(source2, RIM, 1, lambda: edge_share(source2, send_v2, recv_v2))
+    edge_wait(source_copies[1])
     sum_sent()
     covariance(source2, lambda part: sum_part(later_part, gathered3, 2, part))
     wide = my_sea() * member_sum(later_part, gathered3, 2) / divisor
@@ -516,7 +548,7 @@
             vmem((3, ext, 384), F32),
             vmem((LANES, count), BF16),
             vmem((places // 4, tile_cols, 4 * q * LANES), BF16),
-        ] + [dma((8,))] * 10 + [dma((6, 2)), dma((2, 2))],
+        ] + [dma((8,))] * 6 + [dma((8 * mem_size,)), dma((8,))] * 2 + [dma((6, 2)), dma((2, 2))],
         compiler_params=pltpu.CompilerParams(
             collective_id=0, has_side_effects=True, vmem_limit_bytes=40 * 1024 * 1024
         ),

time: 54 us -> 52.2 us (0.967)
  Pallas kernels: 50.7 us -> 48.9 us
    pallas_call x1, Pallas kernels: 50.7 us -> 48.9 us  [per_device(): pl.pallas_call(functools.partial(kernel, (lat_size, lon_size, mem_size, p...]
where the time goes in v6:
time: 52.2 us; the launch traced here: 52.1 us
  Pallas kernels  48.9 us (94%)
  local copies, waits for them, and re-layouts  1.26 us (2%)
  other arithmetic  1.16 us (2%)
  between operations  0.75 us (1%)
    pallas_call x1, Pallas kernels, per_device(): pl.pallas_call(functools.partial(kernel, (lat_size, lon_size, mem_size, p...  48.9 us
    unnamed x16, local copies, waits for them, and re-layouts  1.26 us
    convert_element_type x1, other arithmetic, per_device(): member_rows = jnp.transpose(perturbations, (1, 0, 2)).astype(F32)  1.16 us

profile of v6, /device:TPU:0, one launch (start us, length us, event | category | flops | bytes accessed | tf_op | source)
XLA Modules:
  0.0 52.1 jit_solution(5341975465601731972)
XLA Ops:
  0.6 0.0 copy-start
  0.6 0.0 copy-start.1
  0.7 0.0 copy-start.2
  0.7 0.0 copy-start.3
  0.7 0.0 copy-start.4
  0.7 0.0 copy-start.5
  0.7 0.0 copy-start.6
  0.7 1.2 %convert_bitcast_fusion.member_ref = f32[64,8,256]{2,1,0:T(8,128)S(1)} fusion(bf16[8,64,256]{2,1,0:T(8,128)(2,1)} %plain_ref.1), kind=kLoop, calls=%fused_computation | loop fusion | flops 131072 | bytes 786432 | tf_op jit(solution)/shard_map/convert_element_type | solution.py:517
  1.9 0.0 copy-done
  1.9 0.0 copy-done.1
  1.9 0.0 copy-done.2
  1.9 0.0 copy-done.3
  1.9 0.0 copy-done.4
  1.9 0.0 copy-done.5
  1.9 0.0 copy-done.6
  1.9 48.9 %update.1 = (f32[64,256]{1,0:T(8,128)S(1)}, f32[16,128]{1,0:T(8,128)S(1)}) custom-call(f32[64,8,256]{2,1,0:T(8,128)S(1)} %convert_bitcast_fusion.member_ref, bf16[8,64,256]{2,1,0:T(8,128)(2,1)S(1)} %copy-done, f32[64,256]{1,0:T(8,128)S(1)} %copy-done.1, s32[64,256]{1,0:T(8,128)S(1)} %copy-done.2, s32[16,128]{1,0:T(8,128)S(1)} %bitcast.8, ...), custom_call_target="tpu_custom_call" | custom-call | tf_op jit(solution)/shard_map/update/pallas_call | solution.py:518
  50.8 0.6 %copy.13 = f32[64,256]{1,0:T(8,128)} copy(f32[64,256]{1,0:T(8,128)S(1)} %get-tuple-element.8) | data formatting | bytes 131072
  51.5 0.6 %copy.14 = f32[2048]{0:T(1024)} copy(f32[2048]{0:T(1024)S(1)} %bitcast.7) | data formatting | bytes 16384
Async XLA Ops:
  0.6 1.2 %copy-start = (bf16[8,64,256]{2,1,0:T(8,128)(2,1)S(1)}, bf16[8,64,256]{2,1,0:T(8,128)(2,1)}, u32[]{:S(2)}) copy-start(bf16[8,64,256]{2,1,0:T(8,128)(2,1)} %plain_ref.1) | copy-start | bytes 786436
  0.6 1.2 %copy-start.1 = (f32[64,256]{1,0:T(8,128)S(1)}, f32[64,256]{1,0:T(8,128)}, u32[]{:S(2)}) copy-start(f32[64,256]{1,0:T(8,128)} %rate_ref.1) | copy-start | bytes 196612
  0.7 1.2 %copy-start.2 = (s32[64,256]{1,0:T(8,128)S(1)}, s32[64,256]{1,0:T(8,128)}, u32[]{:S(2)}) copy-start(s32[64,256]{1,0:T(8,128)} %sea_ref.1) | copy-start | bytes 196612
  0.7 1.2 %copy-start.3 = (s32[2048,1]{0,1:T(1,128)S(1)}, s32[2048,1]{0,1:T(1,128)}, u32[]{:S(2)}) copy-start(s32[2048,1]{0,1:T(1,128)} %param.10) | copy-start | bytes 24580
  0.7 1.2 %copy-start.4 = (s32[2048]{0:T(1024)S(1)}, s32[2048]{0:T(1024)}, u32[]{:S(2)}) copy-start(s32[2048]{0:T(1024)} %param.11) | copy-start | bytes 24580
  0.7 1.2 %copy-start.5 = (f32[2048]{0:T(1024)S(1)}, f32[2048]{0:T(1024)}, u32[]{:S(2)}) copy-start(f32[2048]{0:T(1024)} %param.12) | copy-start | bytes 24580
  0.7 1.2 %copy-start.6 = (f32[2048]{0:T(1024)S(1)}, f32[2048]{0:T(1024)}, u32[]{:S(2)}) copy-start(f32[2048]{0:T(1024)} %param.13) | copy-start | bytes 24580

commit v7 on v6

--- a/solution.py
+++ b/solution.py
@@ -44,11 +44,11 @@
 
 def kernel(
     sizes,
-    member_ref, plain_ref, rate_ref, sea_ref, owner_ref, cell_ref, depart_ref, weight_ref,
+    plain_ref, rate_ref, sea_ref, owner_ref, cell_ref, depart_ref, weight_ref,
     increment_ref, residual_ref,
     member_all, edge_ext, coef_ext, source1, source2, spread, north_all, east_all, west_all,
     outgoing, arrived, partial1, partial, gathered1, gathered2, gathered3, kept, answers, returned,
-    rank_ref, total_ref, wide_ref, lane_hot, column_hot,
+    rank_ref, total_ref, wide_ref, lane_hot, column_hot, plain_wide,
     send_x, recv_x, send_e, recv_e, send_c, recv_c, send_v1, recv_v1, send_v2, recv_v2, sums_sem, a2a_sem,
 ):
     lat_size, lon_size, mem_size, places, q, block_rows, divisor = sizes
@@ -118,7 +118,6 @@
 
     member_all[0:4, :, 0:tile_cols] = jnp.zeros((4, 8, tile_cols), F32)
     member_all[end + 4 : ext_rows, :, 0:tile_cols] = jnp.zeros((4, 8, tile_cols), F32)
-    member_all[RIM:end, :, 0:tile_cols] = member_ref[...]
     lane = lax.broadcasted_iota(jnp.int32, (1, LANES), 1)
     edges = jnp.zeros((tile_rows, LANES), F32)
     for m in range(8):
@@ -246,6 +245,22 @@
     exchange(outgoing, arrived, a2a_sem.at[0])
     halo_start(coef_copies)
     halo_start(edge_copies)
+    for m in range(8):
+        for half in range(2):
+            plain_wide[half, m * tile_rows : (m + 1) * tile_rows, :] = plain_ref[
+                m, :, half * LANES : (half + 1) * LANES
+            ].astype(F32)
+
+    def turn_rows(step, carry):
+        for u in range(16):
+            i = step * 16 + u
+            for half in range(2):
+                member_all[RIM + i, :, half * LANES : (half + 1) * LANES] = plain_wide[
+                    half, pl.ds(i, 8, stride=tile_rows), :
+                ]
+        return carry
+
+    lax.fori_loop(0, tile_rows // 16, turn_rows, 0)
     halo_start(member_copies)
     arrived[place] = outgoing[place]
     exchange_wait(outgoing, arrived, a2a_sem.at[0])
@@ -347,31 +362,21 @@
         whole.wait_recv()
         sent.append(whole.wait_send)
 
-    first_part = lambda rows: partial1.at[:, rows]
-    for step in range(1, mem_size):
-        sum_copy(first_part, gathered1, 0, lax.rem(mem + step, mem_size)).start()
-    summed = member_sum(first_part, gathered1, 0)
-    kept[...] = summed
-    source1[pl.ds(RIM + my_rows, quarter), 0:tile_cols] = summed[0]
-
     width = 384
 
     def joined(value):
         side = jnp.where(lane < 64, value[..., 256:384], value[..., 384:512])
         return jnp.concatenate([value[..., 0:256], side], axis=-1)
 
-    def prepare():
-        edge_share(source1, send_v1, recv_v1)
+    def face_weights():
         halo_wait(coef_copies)
-        halo_wait(edge_copies)
-        halo_wait(member_copies)
         rate = joined(coef_ext[0])
         sea = joined(coef_ext[1])
         below = lambda a: jnp.concatenate([a[1:], a[:1]], axis=0)
         wide_ref[0] = 0.5 * (rate + below(rate)) * sea * below(sea)
-        wide_ref[1] = 0.5 * (rate + pltpu.roll(rate, width - 1, 1)) * sea * pltpu.roll(sea, width - 1, 1)
-
-        wide_ref[2] = pltpu.roll(wide_ref[1], 1, 1)
+        east = 0.5 * (rate + pltpu.roll(rate, width - 1, 1)) * sea * pltpu.roll(sea, width - 1, 1)
+        wide_ref[1] = east
+        wide_ref[2] = pltpu.roll(east, 1, 1)
 
         def widen(step, carry):
             base = pl.multiple_of(step * 8, 8)
@@ -380,6 +385,19 @@
                 north_all[i] = jnp.broadcast_to(wide_ref[0, pl.ds(i, 1), :], (8, width))
                 east_all[i] = jnp.broadcast_to(wide_ref[1, pl.ds(i, 1), :], (8, width))
                 west_all[i] = jnp.broadcast_to(wide_ref[2, pl.ds(i, 1), :], (8, width))
+            return carry
+
+        lax.fori_loop(0, ext_rows // 8, widen, 0)
+
+    def prepare():
+        edge_share(source1, send_v1, recv_v1)
+        halo_wait(edge_copies)
+        halo_wait(member_copies)
+
+        def place_sides(step, carry):
+            base = pl.multiple_of(step * 16, 16)
+            for u in range(16):
+                i = base + u
                 line = edge_ext[pl.ds(i, 1), :]
                 both = jnp.where(lax.bitwise_and(lane, 7) < 4, line[:, 128:256], line[:, 256:384])
                 member_all[i, :, 256:384] = pltpu.roll(
@@ -387,7 +405,15 @@
                 )
             return carry
 
-        lax.fori_loop(0, ext_rows // 8, widen, 0)
+        lax.fori_loop(0, ext_rows // 16, place_sides, 0)
+
+    first_part = lambda rows: partial1.at[:, rows]
+    for step in range(1, mem_size):
+        sum_copy(first_part, gathered1, 0, lax.rem(mem + step, mem_size)).start()
+    face_weights()
+    summed = member_sum(first_part, gathered1, 0)
+    kept[...] = summed
+    source1[pl.ds(RIM + my_rows, quarter), 0:tile_cols] = summed[0]
 
     member_share(source1, RIM, 0, prepare)
     edge_wait(source_copies[0])
@@ -514,14 +540,13 @@
     vmem = pltpu.VMEM
     dma = pltpu.SemaphoreType.DMA
     as_rows = lambda a: a.reshape(rows, LANES)
-    member_rows = jnp.transpose(perturbations, (1, 0, 2)).astype(F32)
     increment, residual = pl.pallas_call(
         functools.partial(kernel, (lat_size, lon_size, mem_size, places, q, block_rows, divisor)),
         out_shape=(
             jax.ShapeDtypeStruct((tile_rows, tile_cols), F32),
             jax.ShapeDtypeStruct((rows, LANES), F32),
         ),
-        in_specs=[pl.BlockSpec(memory_space=vmem)] * 8,
+        in_specs=[pl.BlockSpec(memory_space=vmem)] * 7,
         out_specs=(pl.BlockSpec(memory_space=vmem),) * 2,
         scratch_shapes=[
             vmem((ext, 8, 384), F32),
@@ -548,13 +573,14 @@
             vmem((3, ext, 384), F32),
             vmem((LANES, count), BF16),
             vmem((places // 4, tile_cols, 4 * q * LANES), BF16),
+            vmem((2, 8 * tile_rows, LANES), F32),
         ] + [dma((8,))] * 6 + [dma((8 * mem_size,)), dma((8,))] * 2 + [dma((6, 2)), dma((2, 2))],
         compiler_params=pltpu.CompilerParams(
             collective_id=0, has_side_effects=True, vmem_limit_bytes=40 * 1024 * 1024
         ),
         name="update",
     )(
-        member_rows, perturbations, diffusivity, sea_mask,
+        perturbations, diffusivity, sea_mask,
         as_rows(obs_owner), as_rows(obs_cell), as_rows(obs_depart), as_rows(obs_weight),
     )
     return increment, residual.reshape(count)

time: 52.2 us -> 56.3 us (1.079)
  local copies, waits for them, and re-layouts: 1.26 us -> 6.64 us
  other arithmetic: 1.16 us -> 0 us
    unnamed x16, local copies, waits for them, and re-layouts: 1.26 us -> 6.64 us
    convert_element_type x1 -> x0, other arithmetic: 1.16 us -> none  [per_device(): member_rows = jnp.transpose(perturbations, (1, 0, 2)).astype(F32)]
where the time goes in v7:
time: 56.3 us; the launch traced here: 55.9 us
  Pallas kernels  48.6 us (86%)
  local copies, waits for them, and re-layouts  6.64 us (12%)
  between operations  0.66 us (1%)
    pallas_call x1, Pallas kernels, per_device(): pl.pallas_call(functools.partial(kernel, (lat_size, lon_size, mem_size, p...  48.6 us
    unnamed x16, local copies, waits for them, and re-layouts  6.64 us

profile of v7, /device:TPU:0, one launch (start us, length us, event | category | flops | bytes accessed | tf_op | source)
XLA Modules:
  0.0 55.9 jit_solution(12032894963118985336)
XLA Ops:
  0.6 0.0 copy-start
  0.6 0.9 %copy-done = bf16[8,64,256]{2,1,0:T(8,128)(2,1)S(1)} copy-done((bf16[8,64,256]{2,1,0:T(8,128)(2,1)S(1)}, bf16[8,64,256]{2,1,0:T(8,128)(2,1)}, u32[]{:S(2)}) %copy-start) | copy-done | bytes 262168
  1.6 0.0 copy-start.1
  1.6 0.8 %copy-done.1 = f32[64,256]{1,0:T(8,128)S(1)} copy-done((f32[64,256]{1,0:T(8,128)S(1)}, f32[64,256]{1,0:T(8,128)}, u32[]{:S(2)}) %copy-start.1) | copy-done | bytes 65560
  2.4 0.0 copy-start.2
  2.4 0.8 %copy-done.2 = s32[64,256]{1,0:T(8,128)S(1)} copy-done((s32[64,256]{1,0:T(8,128)S(1)}, s32[64,256]{1,0:T(8,128)}, u32[]{:S(2)}) %copy-start.2) | copy-done | bytes 65560
  3.3 0.0 copy-start.3
  3.3 0.7 %copy-done.3 = s32[2048,1]{0,1:T(1,128)S(1)} copy-done((s32[2048,1]{0,1:T(1,128)S(1)}, s32[2048,1]{0,1:T(1,128)}, u32[]{:S(2)}) %copy-start.3) | copy-done | bytes 8216
  4.0 0.0 copy-start.4
  4.0 0.7 %copy-done.4 = s32[2048]{0:T(1024)S(1)} copy-done((s32[2048]{0:T(1024)S(1)}, s32[2048]{0:T(1024)}, u32[]{:S(2)}) %copy-start.4) | copy-done | bytes 8216
  4.7 0.0 copy-start.5
  4.7 0.7 %copy-done.5 = f32[2048]{0:T(1024)S(1)} copy-done((f32[2048]{0:T(1024)S(1)}, f32[2048]{0:T(1024)}, u32[]{:S(2)}) %copy-start.5) | copy-done | bytes 8216
  5.4 0.0 copy-start.6
  5.4 0.7 %copy-done.6 = f32[2048]{0:T(1024)S(1)} copy-done((f32[2048]{0:T(1024)S(1)}, f32[2048]{0:T(1024)}, u32[]{:S(2)}) %copy-start.6) | copy-done | bytes 8216
  6.1 48.6 %update.1 = (f32[64,256]{1,0:T(8,128)S(1)}, f32[16,128]{1,0:T(8,128)S(1)}) custom-call(bf16[8,64,256]{2,1,0:T(8,128)(2,1)S(1)} %copy-done, f32[64,256]{1,0:T(8,128)S(1)} %copy-done.1, s32[64,256]{1,0:T(8,128)S(1)} %copy-done.2, s32[16,128]{1,0:T(8,128)S(1)} %bitcast.6, s32[16,128]{1,0:T(8,128)S(1)} %bitcast.7, f32[16,128]{1,0:T(8,128)S(1)} %bitcast.8, ...), custom_call_target="tpu_custom_call" | custom-call | tf_op jit(solution)/shard_map/update/pallas_call | solution.py:543
  54.7 0.6 %copy.11 = f32[64,256]{1,0:T(8,128)} copy(f32[64,256]{1,0:T(8,128)S(1)} %get-tuple-element.8) | data formatting | bytes 131072
  55.3 0.6 %copy.12 = f32[2048]{0:T(1024)} copy(f32[2048]{0:T(1024)S(1)} %bitcast.5) | data formatting | bytes 16384
Async XLA Ops:
  0.6 1.0 %copy-start = (bf16[8,64,256]{2,1,0:T(8,128)(2,1)S(1)}, bf16[8,64,256]{2,1,0:T(8,128)(2,1)}, u32[]{:S(2)}) copy-start(bf16[8,64,256]{2,1,0:T(8,128)(2,1)} %plain_ref.1) | copy-start | bytes 786436
  1.6 0.8 %copy-start.1 = (f32[64,256]{1,0:T(8,128)S(1)}, f32[64,256]{1,0:T(8,128)}, u32[]{:S(2)}) copy-start(f32[64,256]{1,0:T(8,128)} %rate_ref.1) | copy-start | bytes 196612
  2.4 0.8 %copy-start.2 = (s32[64,256]{1,0:T(8,128)S(1)}, s32[64,256]{1,0:T(8,128)}, u32[]{:S(2)}) copy-start(s32[64,256]{1,0:T(8,128)} %sea_ref.1) | copy-start | bytes 196612
  3.3 0.7 %copy-start.3 = (s32[2048,1]{0,1:T(1,128)S(1)}, s32[2048,1]{0,1:T(1,128)}, u32[]{:S(2)}) copy-start(s32[2048,1]{0,1:T(1,128)} %param.10) | copy-start | bytes 24580
  4.0 0.7 %copy-start.4 = (s32[2048]{0:T(1024)S(1)}, s32[2048]{0:T(1024)}, u32[]{:S(2)}) copy-start(s32[2048]{0:T(1024)} %param.11) | copy-start | bytes 24580
  4.7 0.7 %copy-start.5 = (f32[2048]{0:T(1024)S(1)}, f32[2048]{0:T(1024)}, u32[]{:S(2)}) copy-start(f32[2048]{0:T(1024)} %param.12) | copy-start | bytes 24580
  5.4 0.7 %copy-start.6 = (f32[2048]{0:T(1024)S(1)}, f32[2048]{0:T(1024)}, u32[]{:S(2)}) copy-start(f32[2048]{0:T(1024)} %param.13) | copy-start | bytes 24580
